TPU v7x, 32 devices: a whole 2x2x4 slice. The times are simulated.
32 devices in a mesh: fsdp: 32 (over z, y, x, core).
Axes of the slice: x: 2, y: 2, z: 4, core: 2. Of those that a mesh axis runs over, the one named last changes fastest.
Arguments:
- tokens: bfloat16 [12608, 768], P('fsdp'), may hold values from -6 to 6
- ln1_gain: bfloat16 [768], P('fsdp'), may hold values from 0.5 to 1.5
- ln1_shift: bfloat16 [768], P('fsdp'), may hold values from -3 to 3
- qkv_weight: bfloat16 [768, 2304], P('fsdp'), may hold values from -0.21875 to 0.21875
- qv_bias: bfloat16 [2, 768], P(None, 'fsdp'), may hold values from -3 to 3
- proj_weight: bfloat16 [768, 768], P('fsdp'), may hold values from -1 to 1
- proj_bias: bfloat16 [768], P('fsdp'), may hold values from -3 to 3
- ln2_gain: bfloat16 [768], P('fsdp'), may hold values from 0.5 to 1.5
- ln2_shift: bfloat16 [768], P('fsdp'), may hold values from -3 to 3
- router_weight: bfloat16 [768, 4], P('fsdp'), may hold values from -0.15625 to 0.15625
- expert_in: bfloat16 [3072, 4, 768], P('fsdp'), may hold values from -0.21875 to 0.21875
- expert_in_bias: bfloat16 [3072, 4], P('fsdp'), may hold values from -3 to 3
- expert_out: bfloat16 [3072, 4, 768], P('fsdp'), may hold values from -0.3125 to 0.3125
- expert_out_bias: bfloat16 [4, 768], P(None, 'fsdp'), may hold values from -3 to 3
- routes: int32 [12608, 2], P('fsdp'), may hold values from 0 to 3, all different within a row; in each aligned block of 394 rows (0 to 393, 394 to 787, ...) at most 246 rows name the same one
- out_grad: bfloat16 [12608, 768], P('fsdp'), may hold values from -6 to 6
Outputs:
- block_out: bfloat16 [12608, 768], P('fsdp')
- tokens_grad: float32 [12608, 768], P('fsdp')
- ln1_gain_grad: float32 [768], P('fsdp')
- ln1_shift_grad: float32 [768], P('fsdp')
- qkv_weight_grad: float32 [768, 2304], P('fsdp')
- qv_bias_grad: float32 [2, 768], P(None, 'fsdp')
- proj_weight_grad: float32 [768, 768], P('fsdp')
- proj_bias_grad: float32 [768], P('fsdp')
- ln2_gain_grad: float32 [768], P('fsdp')
- ln2_shift_grad: float32 [768], P('fsdp')
- router_weight_grad: float32 [768, 4], P('fsdp')
- expert_in_grad: float32 [3072, 4, 768], P('fsdp')
- expert_in_bias_grad: float32 [3072, 4], P('fsdp')
- expert_out_grad: float32 [3072, 4, 768], P('fsdp')
- expert_out_bias_grad: float32 [4, 768], P(None, 'fsdp')
Inputs may be any that keep to these rules, and one draw needn't show every extreme that they name: `routes`: each row names 2 different experts. Within the rows of one device no expert is named more than 246 times, and in some blocks one expert is named exactly 246 times.
All inputs are finite; a program needn't handle non-finite values.
Results may differ from a plain program's by a relative error of at most 0.015.
Values may be sent and summed in bfloat16 or wider, within the bound.
A program may use at most 320 MiB of HBM per device.

v0:
```python
import functools

import jax
import jax.numpy as jnp
from jax import lax
from jax.experimental import pallas as pl
from jax.experimental.pallas import tpu as pltpu
from jax.sharding import PartitionSpec as P

HEADS = 12
HD = 64
EXPERTS = 4
TOP = 2
LEN = 197
SEQ_DEV = 2
SLOTS = 256
PLANE = 2 * EXPERTS
LANES = 128


def layer_norm(values, gain_vec, shift_vec):
    row_mean = jnp.mean(values, axis=-1, keepdims=True)
    centred = values - row_mean
    spread = jnp.mean(centred * centred, axis=-1, keepdims=True)
    return centred * lax.rsqrt(spread + 1e-06) * gain_vec + shift_vec


def gelu_tanh(values):
    return jax.nn.gelu(values, approximate=True)


def take_columns(block, widths):
    pieces, at = [], 0
    for width in widths:
        pieces.append(block[:, at : at + width])
        at += width
    return pieces


def dot_f32(left, right, left_dim, right_dim):
    return lax.dot_general(
        left,
        right,
        (((left_dim,), (right_dim,)), ((), ())),
        preferred_element_type=jnp.float32,
    )


def to_chip(array, k, n_dev):
    return lax.ppermute(array, "fsdp", [(i, i ^ (2 * k)) for i in range(n_dev)])


def to_core(array, n_dev):
    return lax.ppermute(array, "fsdp", [(i, i ^ 1) for i in range(n_dev)])


def along_line(array, step, n_dev, first, last):
    pairs = [
        (i, i + step * PLANE) for i in range(n_dev) if first <= i // PLANE <= last
    ]
    return lax.ppermute(array, "fsdp", pairs)


def around_line(array, shift, n_dev):
    return lax.ppermute(array, "fsdp", [(i, (i + shift * PLANE) % n_dev) for i in range(n_dev)])


def after(value, *others):
    return lax.optimization_barrier((value,) + others)[0]


def place():
    here = lax.axis_index("fsdp")
    return here % 2, (here // 2) % EXPERTS, here // PLANE


def chip_apart(chip, k):
    x, y = chip % 2, chip // 2
    x = 1 - x if k % 2 else x
    y = 1 - y if k // 2 else y
    return 2 * y + x


def entry_barrier(planes, chips):
    core, chip, plane = place()
    barrier = pltpu.get_barrier_semaphore()
    mesh = pl.DeviceIdType.MESH

    def greet(device):
        pl.semaphore_signal(barrier, inc=1, device_id=(device,), device_id_type=mesh)

    greet(plane * PLANE + chip * 2 + 1 - core)
    for k in chips:
        greet(plane * PLANE + chip_apart(chip, k) * 2 + core)

    greet((plane + 1) % planes * PLANE + chip * 2 + core)
    greet((plane + planes - 1) % planes * PLANE + chip * 2 + core)
    pl.semaphore_wait(barrier, 3 + len(chips))


def remote(src, dst, send, recv, device):
    return pltpu.make_async_remote_copy(
        src_ref=src,
        dst_ref=dst,
        send_sem=send,
        recv_sem=recv,
        device_id=(device,),
        device_id_type=pl.DeviceIdType.MESH,
    )


def gather_kernel(
    planes, dense_in, weight_in, dense, weight,
    line_send, line_recv, hop_send, hop_recv, chip_send, chip_recv,
    part_send, part_recv, core_send, core_recv, local,
):
    core, chip, plane = place()
    last = planes - 1
    other = plane * PLANE + chip * 2 + 1 - core
    above = (plane + 1) * PLANE + chip * 2 + core
    below = (plane - 1) * PLANE + chip * 2 + core

    def peer(k):
        return plane * PLANE + chip_apart(chip, k) * 2 + core

    def line(slot, up):
        to = slot + 1 if up else (slot - 1) % planes
        return remote(
            dense.at[0, 0, slot], dense.at[0, 0, to],
            line_send.at[int(up), slot], line_recv.at[to], above if up else below,
        )

    def arrived(slot):
        return remote(
            dense.at[0, 0, slot], dense.at[0, 0, slot],
            line_send.at[0, slot], line_recv.at[slot], other,
        )

    def hop(up):
        to = 1 if up else last
        return remote(
            weight.at[:, 0], weight.at[:, to],
            hop_send.at[int(up)], hop_recv.at[to], above if up else below,
        )

    def hop_arrived(slot):
        return remote(
            weight.at[:, slot], weight.at[:, slot], hop_send.at[0], hop_recv.at[slot], other
        )

    parts = [
        remote(
            weight_in.at[:, chip_apart(chip, k)], weight.at[:, 0, k],
            part_send.at[k], part_recv.at[k], peer(k),
        )
        for k in range(1, EXPERTS)
    ]
    own_dense = pltpu.make_async_copy(dense_in, dense.at[0, 0, 0], local.at[0])
    own_part = pltpu.make_async_copy(weight_in.at[:, chip], weight.at[:, 0, 0], local.at[1])
    own_dense.start()
    own_part.start()
    entry_barrier(planes, (1, 2, 3))
    own_dense.wait()

    @pl.when(plane < last)
    def _():
        line(0, True).start()

    @pl.when(plane > 0)
    def _():
        line(0, False).start()

    for part in parts:
        part.start()

    def direct(slot, k):
        return remote(
            dense.at[0, 0, slot], dense.at[0, k, slot],
            chip_send.at[k, slot], chip_recv.at[k, slot], peer(k),
        )

    def first(slot):
        return 1 + slot % 2

    def onward(slot):
        k = first(slot)
        return remote(
            dense.at[0, k, slot], dense.at[0, 3, slot],
            chip_send.at[3, slot], chip_recv.at[3, slot], peer(3 - k),
        )

    def swap(slot, k):
        return remote(
            dense.at[0, k, slot], dense.at[1, k, slot],
            core_send.at[k, slot], core_recv.at[k, slot], other,
        )

    for d in range(1, planes):
        @pl.when(plane >= d)
        def _(d=d):
            arrived(d).wait_recv()

            @pl.when(plane < last)
            def _():
                line(d, True).start()

        @pl.when(plane <= last - d)
        def _(d=d):
            arrived(planes - d).wait_recv()

            @pl.when(plane > 0)
            def _():
                line(planes - d, False).start()

        if d == 1:
            for k in (1, 2):
                direct(0, k).start()
            swap(0, 0).start()

    for slot in range(1, planes):
        for k in (1, 2):
            direct(slot, k).start()
        swap(slot, 0).start()
    own_part.wait()
    for part in parts:
        part.wait()

    @pl.when(plane < last)
    def _():
        hop(True).start()

    @pl.when(plane > 0)
    def _():
        hop(False).start()

    for slot in range(planes):
        direct(slot, first(slot)).wait_recv()
        onward(slot).start()
        swap(slot, first(slot)).start()
    for slot in range(planes):
        direct(slot, 3 - first(slot)).wait_recv()
        swap(slot, 3 - first(slot)).start()
    for slot in range(planes):
        onward(slot).wait_recv()
        swap(slot, 3).start()
    for slot in range(planes):
        for k in (1, 2):
            direct(slot, k).wait_send()
        onward(slot).wait_send()
        for k in range(EXPERTS):
            swap(slot, k).wait()

    @pl.when(plane < last)
    def _():
        line(0, True).wait_send()
        hop(True).wait_send()
        hop_arrived(last).wait_recv()

    @pl.when(plane > 0)
    def _():
        line(0, False).wait_send()
        hop(False).wait_send()
        hop_arrived(1).wait_recv()

    for d in range(1, planes):
        @pl.when((plane >= d) & (plane < last))
        def _(d=d):
            line(d, True).wait_send()

        @pl.when((plane <= last - d) & (plane > 0))
        def _(d=d):
            line(planes - d, False).wait_send()


def gather_weights(dense_mine, weight_mine, n_dev):
    planes = n_dev // PLANE
    _, _, units, width = weight_mine.shape
    sem = pltpu.SemaphoreType.DMA
    any_spec = pl.BlockSpec(memory_space=pl.ANY)
    return pl.pallas_call(
        functools.partial(gather_kernel, planes),
        out_shape=(
            jax.ShapeDtypeStruct((2, EXPERTS, planes) + dense_mine.shape, dense_mine.dtype),
            jax.ShapeDtypeStruct((2, planes, EXPERTS, units, width), weight_mine.dtype),
        ),
        in_specs=[any_spec] * 2,
        out_specs=(any_spec,) * 2,
        scratch_shapes=[
            sem((2, planes)), sem((planes,)), sem((2,)), sem((planes,)),
            sem((EXPERTS, planes)), sem((EXPERTS, planes)),
            sem((EXPERTS,)), sem((EXPERTS,)),
            sem((EXPERTS, planes)), sem((EXPERTS, planes)), sem((2,)),
        ],
        compiler_params=pltpu.CompilerParams(collective_id=1, has_side_effects=True),
        cost_estimate=pl.CostEstimate(flops=0, bytes_accessed=100_000_000, transcendentals=0),
    )(dense_mine, weight_mine)


def exchange_kernel(
    planes, weight_in, rows, grads, weight, theirs, got_rows, got_grads,
    hop_send, hop_recv, core_send, core_recv, row_send, row_recv, local,
):
    core, chip, plane = place()
    last = planes - 1
    other = plane * PLANE + chip * 2 + 1 - core
    above = (plane + 1) * PLANE + chip * 2 + core
    below = (plane - 1) * PLANE + chip * 2 + core

    def hop(slot, up):
        to = slot + 1 if up else (slot - 1) % planes
        return remote(
            weight.at[:, slot], weight.at[:, to],
            hop_send.at[slot], hop_recv.at[to], above if up else below,
        )

    def hop_arrived(slot):
        return remote(
            weight.at[:, slot], weight.at[:, slot], hop_send.at[slot], hop_recv.at[slot], other
        )

    def swap(slot):
        return remote(
            weight.at[:, slot], theirs.at[:, slot],
            core_send.at[slot], core_recv.at[slot], other,
        )

    keep = [
        pltpu.make_async_copy(rows.at[0], got_rows.at[0], local.at[0]),
        pltpu.make_async_copy(grads.at[0], got_grads.at[0], local.at[1]),
    ]
    for copy in keep:
        copy.start()
    entry_barrier(planes, (1, 2, 3))

    def onward(d, wait):
        @pl.when(plane >= d)
        def _():
            if wait:
                hop_arrived(d).wait_recv()

            @pl.when(plane < last)
            def _():
                hop(d, True).start()

            swap(d).start()

        @pl.when(plane <= last - d)
        def _():
            if wait:
                hop_arrived(planes - d).wait_recv()

            @pl.when(plane > 0)
            def _():
                hop(planes - d, False).start()

            swap(planes - d).start()

    onward(1, False)
    trades = []
    for n, (src, dst) in enumerate(((rows, got_rows), (grads, got_grads))):
        for k in range(1, EXPERTS):
            trades.append(
                remote(
                    src.at[k], dst.at[k], row_send.at[n, k], row_recv.at[n, k],
                    plane * PLANE + chip_apart(chip, k) * 2 + core,
                )
            )
    for trade in trades:
        trade.start()
    swap(0).start()
    for d in range(2, planes):
        onward(d, True)
    for trade in trades:
        trade.wait()
    for copy in keep:
        copy.wait()
    for slot in range(planes):
        swap(slot).wait()
    for d in range(1, planes):
        @pl.when((plane >= d) & (plane < last))
        def _(d=d):
            hop(d, True).wait_send()

        @pl.when((plane <= last - d) & (plane > 0))
        def _(d=d):
            hop(planes - d, False).wait_send()


def exchange_rows(weight, rows, grads, n_dev):
    planes = n_dev // PLANE
    sem = pltpu.SemaphoreType.DMA
    any_spec = pl.BlockSpec(memory_space=pl.ANY)

    def like(array):
        return jax.ShapeDtypeStruct(array.shape, array.dtype)

    return pl.pallas_call(
        functools.partial(exchange_kernel, planes),
        out_shape=(like(weight), like(weight), like(rows), like(grads)),
        in_specs=[any_spec] * 3,
        out_specs=(any_spec,) * 4,
        input_output_aliases={0: 0},
        scratch_shapes=[
            sem((planes,)), sem((planes,)), sem((planes,)), sem((planes,)),
            sem((2, EXPERTS)), sem((2, EXPERTS)), sem((2,)),
        ],
        compiler_params=pltpu.CompilerParams(collective_id=2, has_side_effects=True),
        cost_estimate=pl.CostEstimate(flops=0, bytes_accessed=150_000_000, transcendentals=0),
    )(weight, rows, grads)


def scatter_direct(slots, n_dev):
    total = slots[0].astype(jnp.float32)
    for s in range(1, n_dev // PLANE):
        total = total + around_line(slots[s], -s, n_dev).astype(jnp.float32)
    return total


def sum_low(mine, got):
    return (mine.astype(jnp.float32) + got.astype(jnp.float32)).astype(jnp.bfloat16)


def scatter_start(slots, n_dev):
    if n_dev // PLANE != 4:
        return ()
    return along_line(slots[1], 1, n_dev, 0, 0), along_line(slots[3], -1, n_dev, 3, 3)


def scatter_middle(slots, hops, n_dev):
    if n_dev // PLANE != 4:
        return ()
    up = along_line(sum_low(slots[2], hops[0]), 1, n_dev, 0, 1)
    down = along_line(sum_low(slots[2], hops[1]), -1, n_dev, 2, 3)
    return up, down


def scatter_end(slots, hops, n_dev):
    if n_dev // PLANE != 4:
        return scatter_direct(slots, n_dev)
    up = along_line(sum_low(slots[3], hops[0]), 1, n_dev, 0, 2)
    down = along_line(sum_low(slots[1], hops[1]), -1, n_dev, 1, 3)
    return slots[0].astype(jnp.float32) + up.astype(jnp.float32) + down.astype(jnp.float32)


def on_device(
    n_dev,
    tokens,
    ln1_gain,
    ln1_shift,
    qkv_weight,
    qv_bias,
    proj_weight,
    proj_bias,
    ln2_gain,
    ln2_shift,
    router_weight,
    expert_in,
    expert_in_bias,
    expert_out,
    expert_out_bias,
    routes,
    out_grad,
):
    highest = lax.Precision.HIGHEST
    f32 = jnp.float32
    low = jnp.bfloat16
    row_count, model_width = tokens.shape
    shape_four = (SEQ_DEV, LEN, HEADS, HD)
    query_scale = HD ** (-0.5)
    own = qkv_weight.shape[0]
    units = expert_in.shape[0]
    planes = n_dev // PLANE
    each = range(EXPERTS)
    wide = 4 * model_width
    here = lax.axis_index("fsdp")
    core = here % 2
    chip = (here // 2) % EXPERTS
    plane = here // PLANE

    def owner_dense(j):
        s, k, c = j % planes, (j // planes) % EXPERTS, j // (planes * EXPERTS)
        return ((plane - s + planes) % planes) * PLANE + (chip ^ k) * 2 + (core ^ c)

    def owner_units(j):
        k, s, c = j % EXPERTS, (j // EXPERTS) % planes, j // (planes * EXPERTS)
        return ((plane - s + planes) % planes) * PLANE + (chip ^ k) * 2 + (core ^ c)

    devices = jnp.arange(n_dev, dtype=jnp.int32)
    sort_dense = (devices[:, None] == owner_dense(devices)[None, :]).astype(low)
    sort_units = (devices[:, None] == owner_units(devices)[None, :]).astype(low)
    features = jnp.arange(model_width, dtype=jnp.int32)
    home = owner_dense(features // own) * own + features % own
    sort_rows = (features[:, None] == home[None, :]).astype(low)

    small_parts = [
        ln1_gain,
        ln1_shift,
        qv_bias.reshape(-1),
        proj_bias,
        ln2_gain,
        ln2_shift,
        router_weight.T.reshape(-1),
        expert_out_bias.reshape(-1),
        expert_in_bias.T.reshape(-1),
    ]
    small_widths = [p.shape[0] for p in small_parts]
    small_total = sum(small_widths)
    small_room = own * LANES
    small_mine = jnp.pad(jnp.concatenate(small_parts), (0, small_room - small_total))
    dense_mine = jnp.concatenate(
        [qkv_weight, proj_weight, small_mine.reshape(own, LANES)], axis=1
    )
    weight_mine = jnp.stack([expert_in.transpose(1, 0, 2), expert_out.transpose(1, 0, 2)])
    dense, own_half = gather_weights(dense_mine, weight_mine, n_dev)
    dense = dense.reshape(model_width, wide + LANES)

    w_qkv = dense[:, : 3 * model_width]
    w_proj = dense[:, 3 * model_width : wide]
    small = dense[:, wide:].reshape(n_dev, small_room)
    small = dot_f32(sort_dense, small, 1, 0).astype(low)
    gain1, shift1, bias_qv, bias_proj, gain2, shift2, w_router, bias_out, bias_in = take_columns(
        small, small_widths
    )
    gain1 = gain1.reshape(-1).astype(f32)
    shift1 = shift1.reshape(-1).astype(f32)
    gain2 = gain2.reshape(-1).astype(f32)
    shift2 = shift2.reshape(-1).astype(f32)
    bias_proj = bias_proj.reshape(-1).astype(f32)
    bias_q = bias_qv[:, :own].reshape(-1).astype(f32)
    bias_v = bias_qv[:, own:].reshape(-1).astype(f32)
    w_router = jnp.stack([p.reshape(-1) for p in take_columns(w_router, [own] * EXPERTS)])
    bias_out = jnp.stack([p.reshape(-1) for p in take_columns(bias_out, [own] * EXPERTS)])
    mine = (jnp.arange(EXPERTS, dtype=jnp.int32) == chip).astype(f32)
    bias_out = jnp.sum(bias_out.astype(f32) * mine[:, None], axis=0)
    bias_in = jnp.stack(take_columns(bias_in, [units] * EXPERTS)).astype(f32)
    bias_in = jnp.sum(bias_in * mine[:, None, None], axis=0).astype(low)
    bias_in = dot_f32(sort_units, bias_in, 0, 0).reshape(2, n_dev * units // 2)

    experts = jnp.arange(EXPERTS, dtype=jnp.int32)[None, :]
    pick = [(routes[:, j : j + 1] == experts).astype(f32) for j in range(TOP)]
    picked = pick[0] + pick[1]
    tri = jnp.arange(row_count)[:, None] > jnp.arange(row_count)[None, :]
    before = dot_f32(tri.astype(low), picked.astype(low), 1, 0)
    slot_ids = jnp.arange(EXPERTS * SLOTS, dtype=jnp.int32)[None, :]
    hit = []
    for j in range(TOP):
        slot = jnp.sum(pick[j] * before, axis=1, keepdims=True).astype(jnp.int32)
        hit.append(slot_ids == (routes[:, j : j + 1] ^ chip) * SLOTS + slot)
    dispatch = (hit[0] | hit[1]).astype(low)

    inputs = tokens.astype(f32)
    normed_full, norm1_pull = jax.vjp(layer_norm, inputs, gain1, shift1)
    normed = dot_f32(normed_full.astype(low), sort_rows, 1, 0).astype(low)
    projected = jnp.dot(normed, w_qkv, preferred_element_type=f32)
    queries = ((projected[:, :model_width] + bias_q) * query_scale).astype(low).reshape(shape_four)
    key_rows = projected[:, model_width : 2 * model_width].astype(low).reshape(shape_four)
    values = (projected[:, 2 * model_width :] + bias_v).astype(low).reshape(shape_four)
    scores = jnp.einsum("sqhd,skhd->shqk", queries, key_rows, preferred_element_type=f32)
    exp_scores = jnp.exp(scores - jnp.max(scores, axis=-1, keepdims=True))
    probs_full = exp_scores / jnp.sum(exp_scores, axis=-1, keepdims=True)
    probs_low = probs_full.astype(low)
    attended = jnp.einsum("shqk,skhd->sqhd", probs_low, values, preferred_element_type=f32)
    attended = attended.reshape(row_count, model_width).astype(low)
    attended = dot_f32(attended, sort_rows, 1, 0).astype(low)

    middle = inputs + jnp.dot(attended, w_proj, preferred_element_type=f32) + bias_proj
    normed2_full, norm2_pull = jax.vjp(layer_norm, middle, gain2, shift2)
    normed2 = normed2_full.astype(low)
    gate_probs = jax.nn.softmax(dot_f32(normed2, w_router, 1, 1), axis=-1)
    chosen = [jnp.sum(gate_probs * pick[j], axis=1, keepdims=True) for j in range(TOP)]
    combine = (jnp.where(hit[0], chosen[0], 0.0) + jnp.where(hit[1], chosen[1], 0.0)).astype(low)

    def exchange(rows):
        pieces = [rows[k * SLOTS : (k + 1) * SLOTS] for k in each]
        pieces = [to_chip(p, k, n_dev) if k else p for k, p in enumerate(pieces)]
        return jnp.concatenate(pieces, axis=0)

    four = (EXPERTS, SLOTS, model_width)
    own_half, other_half, slot_rows, grad_result = exchange_rows(
        own_half,
        dot_f32(dispatch, normed2, 0, 0).astype(low).reshape(four),
        dot_f32(combine, out_grad, 0, 0).astype(low).reshape(four),
        n_dev,
    )
    slot_rows = slot_rows.reshape(EXPERTS * SLOTS, model_width)
    grad_result = grad_result.reshape(EXPERTS * SLOTS, model_width)
    halves = [h.reshape(2, n_dev * units // 2, model_width) for h in (own_half, other_half)]
    w_in = [half[0] for half in halves]
    w_out = [half[1] for half in halves]

    hidden, grad_pre, pulls = [], [], []
    for c in range(2):
        pre_act = dot_f32(slot_rows, w_in[c], 1, 1) + bias_in[c]
        out, pull = jax.vjp(gelu_tanh, pre_act)
        hidden.append(out.astype(low))
        pulls.append(pull)
    result = dot_f32(hidden[0], w_out[0], 1, 0) + dot_f32(hidden[1], w_out[1], 1, 0)
    result = exchange((result + bias_out).astype(low))
    for c in range(2):
        grad_pre.append(pulls[c](dot_f32(grad_result, w_out[c], 1, 1))[0].astype(low))
    grad_slots = dot_f32(grad_pre[0], w_in[0], 1, 0) + dot_f32(grad_pre[1], w_in[1], 1, 0)
    grad_slots = exchange(grad_slots.astype(low))

    theirs = jnp.stack(
        [
            dot_f32(grad_pre[1], slot_rows, 0, 0).astype(low),
            dot_f32(hidden[1], grad_result, 0, 0).astype(low),
        ]
    )
    theirs = to_core(theirs, n_dev)
    terms = jnp.stack(
        [dot_f32(grad_pre[0], slot_rows, 0, 0), dot_f32(hidden[0], grad_result, 0, 0)]
    )
    terms = (terms + theirs.astype(f32)).astype(low)
    grad_slots = after(grad_slots, terms)
    result = after(result, terms)
    span = EXPERTS * units
    terms = [terms[:, s * span : (s + 1) * span] for s in range(planes)]
    hops = scatter_start(terms, n_dev)

    grad_bias_in = jnp.concatenate([jnp.sum(g.astype(f32), axis=0) for g in grad_pre])
    grad_bias_in = jnp.dot(
        sort_units.astype(f32), grad_bias_in.reshape(n_dev, units), precision=highest
    )
    grad_bias_in = (mine[None, :, None] * grad_bias_in[:, None, :]).reshape(n_dev, EXPERTS * units)
    grad_bias_out = mine[:, None] * jnp.sum(grad_result.astype(f32), axis=0)[None, :]

    block_out = (middle + jnp.dot(combine, result, preferred_element_type=f32)).astype(low)

    grad_top = out_grad.astype(f32)
    slot_dots = dot_f32(out_grad, result, 1, 1)
    grad_gates = sum(
        pick[j] * jnp.sum(jnp.where(hit[j], slot_dots, 0.0), axis=1, keepdims=True)
        for j in range(TOP)
    )
    grad_logits = gate_probs * (
        grad_gates - jnp.sum(gate_probs * grad_gates, axis=-1, keepdims=True)
    )
    grad_router = jnp.dot(grad_logits.T, normed2.astype(f32), precision=highest)
    grad_normed2 = jnp.dot(grad_logits, w_router.astype(f32), precision=highest)
    grad_normed2 = grad_normed2 + jnp.dot(dispatch, grad_slots, preferred_element_type=f32)
    grad_mid_norm, grad_gain2, grad_shift2 = norm2_pull(grad_normed2)
    grad_middle = grad_top + grad_mid_norm

    grad_branch = grad_middle.astype(low)
    grad_bias_proj = jnp.sum(grad_branch.astype(f32), axis=0)
    grad_proj = dot_f32(attended, grad_branch, 0, 0)
    grad_attended = dot_f32(grad_branch, w_proj, 1, 1).astype(low)
    grad_attended = dot_f32(grad_attended, sort_rows, 1, 1).astype(low).reshape(shape_four)
    grad_probs = jnp.einsum("sqhd,skhd->shqk", grad_attended, values, preferred_element_type=f32)
    grad_values = jnp.einsum(
        "shqk,sqhd->skhd", probs_low, grad_attended, preferred_element_type=f32
    ).astype(low)
    grad_probs = after(grad_probs, *hops)
    hops = scatter_middle(terms, hops, n_dev)
    grad_scores = (
        probs_full * (grad_probs - jnp.sum(probs_full * grad_probs, axis=-1, keepdims=True))
    ).astype(low)
    grad_queries = jnp.einsum(
        "shqk,skhd->sqhd", grad_scores, key_rows, preferred_element_type=f32
    ).astype(low)
    grad_keys = jnp.einsum(
        "shqk,sqhd->skhd", grad_scores, queries, preferred_element_type=f32
    ).astype(low)
    grad_query_pre = grad_queries.astype(f32).reshape(row_count, model_width) * query_scale
    grad_values = grad_values.reshape(row_count, model_width)
    grad_projected = jnp.concatenate(
        [grad_query_pre.astype(low), grad_keys.reshape(row_count, model_width), grad_values],
        axis=1,
    )
    grad_projected = after(grad_projected, *hops)
    expert_mine = scatter_end(terms, hops, n_dev).astype(low)
    grad_qkv = dot_f32(normed, grad_projected, 0, 0)
    grad_normed = dot_f32(grad_projected, w_qkv, 1, 1)
    upper = grad_normed.astype(low)
    lower = (grad_normed - upper.astype(f32)).astype(low)
    grad_normed = dot_f32(upper, sort_rows, 1, 1) + dot_f32(lower, sort_rows, 1, 1)
    grad_in_norm, grad_gain1, grad_shift1 = norm1_pull(grad_normed)
    tokens_grad = grad_middle + grad_in_norm

    def by_owner(rows):
        return rows.reshape(-1, n_dev, rows.shape[-1] // n_dev).transpose(1, 0, 2).reshape(n_dev, -1)

    small_grads = jnp.concatenate(
        [
            by_owner(
                jnp.concatenate(
                    [
                        jnp.stack(
                            [
                                grad_gain1,
                                grad_shift1,
                                jnp.sum(grad_query_pre, axis=0),
                                jnp.sum(grad_values.astype(f32), axis=0),
                                grad_bias_proj,
                                grad_gain2,
                                grad_shift2,
                            ]
                        ),
                        grad_router,
                        grad_bias_out,
                    ],
                    axis=0,
                )
            ),
            grad_bias_in,
        ],
        axis=1,
    ).astype(low)
    small_grads = jnp.pad(small_grads, ((0, 0), (0, small_room - small_total)))
    small_grads = dot_f32(sort_dense, small_grads, 0, 0).astype(low)
    dense_grads = jnp.concatenate(
        [
            grad_qkv.astype(low),
            grad_proj.astype(low),
            small_grads.reshape(n_dev * own, LANES),
        ],
        axis=1,
    )
    half = n_dev * own // 2
    theirs = to_core(dense_grads[half:], n_dev)
    total = (dense_grads[:half].astype(f32) + theirs.astype(f32)).astype(low)
    span = planes * own
    pieces = [total[k * span : (k + 1) * span] for k in each]
    pieces = [to_chip(p, k, n_dev) if k else p for k, p in enumerate(pieces)]
    total = sum(p.astype(f32) for p in pieces).astype(low)
    dense_out = scatter_direct([total[s * own : (s + 1) * own] for s in range(planes)], n_dev)
    pieces = [expert_mine[:, k * units : (k + 1) * units] for k in each]
    pieces = [to_chip(p, k, n_dev) if k else p for k, p in enumerate(pieces)]
    low_bit, high_bit = (chip & 1) == 1, (chip & 2) == 2
    pieces = [jnp.where(low_bit, pieces[k ^ 1], pieces[k]) for k in each]
    pieces = [jnp.where(high_bit, pieces[k ^ 2], pieces[k]) for k in each]
    expert_in_mine, expert_out_mine = [
        jnp.stack([p[w] for p in pieces], axis=1).astype(f32) for w in range(2)
    ]
    small = dense_out[:, wide:].reshape(1, small_room)
    small = [p[0] for p in take_columns(small, small_widths)]
    return (
        block_out,
        tokens_grad,
        small[0],
        small[1],
        dense_out[:, : 3 * model_width],
        small[2].reshape(2, own),
        dense_out[:, 3 * model_width : wide],
        small[3],
        small[4],
        small[5],
        small[6].reshape(EXPERTS, own).T,
        expert_in_mine,
        small[8].reshape(EXPERTS, units).T,
        expert_out_mine,
        small[7].reshape(EXPERTS, own),
    )


def solution(mesh):
    row, flat, wide_row = P("fsdp", None), P("fsdp"), P(None, "fsdp")
    unit = P("fsdp", None, None)
    in_specs = (
        row, flat, flat, row, wide_row, row, flat, flat, flat, row,
        unit, row, unit, wide_row, row, row,
    )
    out_specs = (
        row, row, flat, flat, row, wide_row, row, flat, flat, flat, row,
        unit, row, unit, wide_row,
    )
    return jax.shard_map(
        functools.partial(on_device, mesh.shape["fsdp"]),
        mesh=mesh,
        in_specs=in_specs,
        out_specs=out_specs,
        check_vma=False,
    )
```

profile of v0, /device:TPU:9, one launch (start us, length us, event | category | flops | bytes accessed | tf_op | source)
XLA Modules:
  0.0 466.1 jit_solution(12765009337304969256)
XLA Ops:
  3.8 3.4 concatenate.51
  10.4 48.0 %shard_map.271 = (bf16[2,4,4,24,3200]{4,3,2,1,0:T(8,128)(2,1)}, bf16[2,4,4,96,768]{4,3,2,1,0:T(8,128)(2,1)}) custom-call(bf16[24,3200]{1,0:T(8,128)(2,1)} %pad_maximum_fusion.6.dense_in, bf16[2,4,96,768]{3,2,1,0:T(8,128)(2,1)} %pad_maximum_fusion.5.weight_in), custom_call_target="tpu_custom_call" | custom-call | bytes 100000000 | tf_op jit(solution)/shard_map/pallas_call | solution.py:280
  62.6 3.5 fusion.18
  66.3 2.2 slice.482
  68.4 2.7 fusion.57
  73.4 3.1 reshape.510
  76.6 2.2 copy.56
  78.8 2.1 reshape.511
  80.9 2.2 copy.57
  83.1 3.9 fusion.171
  87.0 3.0 fusion.46
  93.0 2.2 fusion.172
  96.9 2.4 convolution_convert_fusion.6
  99.3 2.5 convolution_convert_fusion.5
  101.8 55.2 %shard_map.272 = (bf16[2,4,4,96,768]{4,3,2,1,0:T(8,128)(2,1)}, bf16[2,4,4,96,768]{4,3,2,1,0:T(8,128)(2,1)}, bf16[4,256,768]{2,1,0:T(8,128)(2,1)}, bf16[4,256,768]{2,1,0:T(8,128)(2,1)}) custom-call(bf16[2,4,4,96,768]{4,3,2,1,0:T(8,128)(2,1)} %get-tuple-element.26.weight_in, bf16[4,256,768]{2,1,0:T(8,128)(2,1)} %bitcast.161, ...), custom_call_target="tpu_custom_call", output_to_operand_aliasing={{0}: (0, {})} | custom-call | bytes 150000000 | tf_op jit(solution)/shard_map/pallas_call | solution.py:397
  157.0 4.9 %fusion.162 = (bf16[1,4,4,96,768]{4,3,2,1,0:T(8,128)(2,1)}, bf16[1,4,4,96,768]{4,3,2,1,0:T(8,128)(2,1)}) fusion(bf16[2,4,4,96,768]{4,3,2,1,0:T(8,128)(2,1)} %get-tuple-element.28), kind=kLoop, calls=%fused_computation.338 | loop fusion | bytes 9437184 | tf_op jit(solution)/shard_map/slice | solution.py:588
  162.3 4.8 %fusion.161 = (bf16[1,4,4,96,768]{4,3,2,1,0:T(8,128)(2,1)}, bf16[1,4,4,96,768]{4,3,2,1,0:T(8,128)(2,1)}) fusion(bf16[2,4,4,96,768]{4,3,2,1,0:T(8,128)(2,1)} %get-tuple-element.29), kind=kLoop, calls=%fused_computation.337 | loop fusion | bytes 9437184 | tf_op jit(solution)/shard_map/slice | solution.py:588
  167.5 7.6 %fusion.175 = f32[1024,1536]{1,0:T(8,128)} fusion(bf16[1024,768]{1,0:T(8,128)(2,1)} %bitcast.196, bf16[1536,768]{1,0:T(8,128)(2,1)} %bitcast.149), kind=kOutput, calls=%fused_computation.351 | convolution fusion | flops 2415919104 | bytes 10223616 | tf_op jit(solution)/shard_map/dot_general | solution.py:41
  175.1 4.5 fusion.176
  179.7 6.9 %fusion.152 = f32[1024,768]{1,0:T(8,128)S(1)} fusion(bf16[1536,768]{1,0:T(8,128)(2,1)} %bitcast.151, f32[1024,1536]{1,0:T(8,128)} %fusion.175, f32[1536]{0:T(1024)S(1)} %add.417), kind=kOutput, calls=%fused_computation.332 | convolution fusion | flops 2431647744 | bytes 11802624 | tf_op jit(solution)/shard_map/dot_general | solution.py:41
  186.7 4.2 add_convert_fusion.2
  192.1 2.6 collective-permute-start
  194.8 4.0 fusion.21
  198.8 6.8 %convert_reduce_fusion = (f32[1536]{0:T(1024)S(1)}, bf16[1024,1536]{1,0:T(8,128)(2,1)S(1)}) fusion(f32[1024,1536]{1,0:T(8,128)S(1)} %copy-done.46, f32[1536]{0:T(1024)S(1)} %add.422, bf16[1024,768]{1,0:T(8,128)(2,1)S(1)} %bitcast.158, bf16[1536,768]{1,0:T(8,128)(2,1)S(1)} %bitcast.156), kind=kOutput, calls=%fused_computation.21 | convolution fusion | flops 2452093440 | bytes 13381632 | tf_op jit(solution)/shard_map/dot_general | solution.py:41
  205.6 3.0 fusion.20
  208.6 2.6 pad_maximum_fusion.1
  211.3 2.5 collective-permute-start.3
  213.8 7.2 %convert_reduce_fusion.1 = (f32[1536]{0:T(1024)S(1)}, bf16[1024,1536]{1,0:T(8,128)(2,1)S(1)}) fusion(f32[1024,1536]{1,0:T(8,128)S(1)} %bitcast.202, f32[1536]{0:T(1024)S(1)} %add.417, bf16[1024,768]{1,0:T(8,128)(2,1)S(1)} %bitcast.159, bf16[1536,768]{1,0:T(8,128)(2,1)S(1)} %bitcast.152), kind=kOutput, calls=%fused_computation.22 | convolution fusion | flops 2452093440 | bytes 13381632 | tf_op jit(solution)/shard_map/dot_general | solution.py:41
  221.0 2.6 fusion.177
  223.6 2.6 add_convert_fusion.1
  227.4 5.4 %convolution_bitcast_fusion = f32[1,1536,768]{2,1,0:T(8,128)} fusion(bf16[1024,768]{1,0:T(8,128)(2,1)S(1)} %bitcast.160, f32[1024,1536]{1,0:T(8,128)S(1)} %bitcast.202, f32[1536]{0:T(1024)S(1)} %add.417), kind=kOutput, calls=%fused_computation.32 | convolution fusion | flops 2431647744 | bytes 12589056 | tf_op jit(solution)/shard_map/dot_general | solution.py:41
  232.8 4.5 convolution_bitcast_fusion.1
  243.9 4.8 %collective-permute-done.5 = bf16[256,768]{1,0:T(8,128)(2,1)} collective-permute-done((bf16[256,768]{1,0:T(8,128)(2,1)}, bf16[256,768]{1,0:T(8,128)(2,1)}, u32[]{:S(2)}, u32[]{:S(2)}) %collective-permute-start.5) | collective-permute-done | bytes 393248 | tf_op jit(solution)/shard_map/ppermute | solution.py:50
  249.5 2.5 pad_maximum_fusion.4
  252.0 6.2 %fusion.1 = bf16[2,1536,768]{2,1,0:T(8,128)(2,1)S(1)} fusion(f32[1,1536,768]{2,1,0:T(8,128)} %convolution_bitcast_fusion, f32[1,1536,768]{2,1,0:T(8,128)} %convolution_bitcast_fusion.1, bf16[2,1536,768]{2,1,0:T(8,128)(2,1)} %collective-permute-done.3), kind=kLoop, calls=%fused_computation.2 | loop fusion | flops 9437184 | bytes 18874368 | tf_op jit(solution)/shard_map/convert_element_type | solution.py:614
  266.1 3.4 fusion.45
  269.5 2.3 reshape.512
  271.8 1.9 copy.62
  276.8 3.6 fusion.174
  283.4 3.1 convolution_convert_fusion.7
  286.5 3.1 fusion.178
  289.6 15.9 %collective-permute-done.7 = bf16[2,384,768]{2,1,0:T(8,128)(2,1)} collective-permute-done((bf16[2,384,768]{2,1,0:T(8,128)(2,1)}, bf16[2,384,768]{2,1,0:T(8,128)(2,1)}, u32[]{:S(2)}, u32[]{:S(2)}) %collective-permute-start.7) | collective-permute-done | bytes 1179680 | tf_op jit(solution)/shard_map/ppermute | solution.py:61
  305.5 6.1 %copy.65 = f32[2,12,197,197]{2,3,1,0:T(8,128)} copy(f32[2,12,197,197]{3,2,1,0:T(8,128)} %fusion.178) | data formatting | bytes 7451328 | tf_op jit(solution)/shard_map/optimization_barrier | solution.py:69
  311.6 4.8 %multiply_reduce_fusion = f32[2,12,197]{2,1,0:T(8,128)S(1)} fusion(f32[2,12,197,197]{2,3,1,0:T(8,128)} %copy.65, f32[2,12,197,197]{2,3,1,0:T(8,128)} %get-tuple-element.165, f32[2,12,197]{2,1,0:T(8,128)S(1)} %get-tuple-element.164), kind=kLoop, calls=%fused_computation.29 | loop fusion | flops 2789520 | bytes 7489152 | tf_op jit(solution)/shard_map/reduce_sum | solution.py:657
  316.4 4.1 fusion.23
  320.5 2.4 collective-permute-start.9
  327.8 3.2 reshape.497
  334.5 13.8 %collective-permute-done.9 = bf16[2,384,768]{2,1,0:T(8,128)(2,1)} collective-permute-done((bf16[2,384,768]{2,1,0:T(8,128)(2,1)}, bf16[2,384,768]{2,1,0:T(8,128)(2,1)}, u32[]{:S(2)}, u32[]{:S(2)}) %collective-permute-start.9) | collective-permute-done | bytes 1179680 | tf_op jit(solution)/shard_map/ppermute | solution.py:61
  348.3 1.9 collective-permute-done.10
  350.3 4.1 fusion.16
  354.3 3.9 convolution_convert_fusion
  362.1 4.4 add_convert_fusion.5
  368.4 3.4 collective-permute-start.18
  375.4 3.9 collective-permute-start.11
  379.3 3.3 fusion.42
  382.6 10.3 %collective-permute-done.19 = bf16[2,384,768]{2,1,0:T(8,128)(2,1)} collective-permute-done((bf16[2,384,768]{2,1,0:T(8,128)(2,1)}, bf16[2,384,768]{2,1,0:T(8,128)(2,1)}, u32[]{:S(2)}, u32[]{:S(2)}) %collective-permute-start.19) | collective-permute-done | bytes 1179680 | tf_op jit(solution)/shard_map/ppermute | solution.py:61
  394.8 2.4 add_convert_fusion.3
  401.6 2.3 collective-permute-done.20
  403.9 7.7 %collective-permute-done.21 = bf16[2,96,768]{2,1,0:T(8,128)(2,1)S(1)} collective-permute-done((bf16[2,96,768]{2,1,0:T(8,128)(2,1)S(1)}, bf16[2,96,768]{2,1,0:T(8,128)(2,1)S(1)}, u32[]{:S(2)}, u32[]{:S(2)}) %collective-permute-start.21) | collective-permute-done | bytes 294944 | tf_op jit(solution)/shard_map/ppermute | solution.py:50
  411.8 2.4 add_convert_fusion
  417.1 11.2 %collective-permute-done.14 = bf16[96,3200]{1,0:T(8,128)(2,1)S(1)} collective-permute-done((bf16[96,3200]{1,0:T(8,128)(2,1)S(1)}, bf16[96,3200]{1,0:T(8,128)(2,1)S(1)}, u32[]{:S(2)}, u32[]{:S(2)}) %collective-permute-start.14) | collective-permute-done | bytes 614432 | tf_op jit(solution)/shard_map/ppermute | solution.py:50
  428.3 15.9 %collective-permute-done.13 = bf16[96,3200]{1,0:T(8,128)(2,1)S(1)} collective-permute-done((bf16[96,3200]{1,0:T(8,128)(2,1)S(1)}, bf16[96,3200]{1,0:T(8,128)(2,1)S(1)}, u32[]{:S(2)}, u32[]{:S(2)}) %collective-permute-start.13) | collective-permute-done | bytes 614432 | tf_op jit(solution)/shard_map/ppermute | solution.py:50
  451.7 6.5 %collective-permute-done.16 = bf16[24,3200]{1,0:T(8,128)(2,1)S(1)} collective-permute-done((bf16[24,3200]{1,0:T(8,128)(2,1)S(1)}, bf16[24,3200]{1,0:T(8,128)(2,1)S(1)}, u32[]{:S(2)}, u32[]{:S(2)}) %collective-permute-start.16) | collective-permute-done | bytes 153632 | tf_op jit(solution)/shard_map/ppermute | solution.py:65
  458.2 2.6 collective-permute-done.15
  (295 shorter events, 81.1 us)
Async XLA Ops:
  0.7 58.8 %copy-start.42 = (s32[32]{0:T(128)}, s32[32]{0:T(128)S(1)}, u32[]{:S(2)}) copy-start(s32[32]{0:T(128)S(1)} %get-tuple-element.176) | copy-start | bytes 388
  8.6 51.5 %copy-start.3 = (bf16[394,768]{1,0:T(8,128)(2,1)S(1)}, bf16[394,768]{1,0:T(8,128)(2,1)}, u32[]{:S(2)}) copy-start(bf16[394,768]{1,0:T(8,128)(2,1)} %param.16) | copy-start | bytes 1815556
  60.4 5.7 %copy-start.33 = (f32[394]{0:T(512)}, f32[394]{0:T(512)S(1)}, u32[]{:S(2)}) copy-start(f32[394]{0:T(512)S(1)} %broadcast_multiply_fusion.1) | copy-start | bytes 4732
  60.7 5.4 %copy-start.36 = (f32[394]{0:T(512)}, f32[394]{0:T(512)S(1)}, u32[]{:S(2)}) copy-start(f32[394]{0:T(512)S(1)} %fusion.54) | copy-start | bytes 4732
  60.7 5.3 %copy-start.38 = (f32[394]{0:T(512)}, f32[394]{0:T(512)S(1)}, u32[]{:S(2)}) copy-start(f32[394]{0:T(512)S(1)} %fusion.131) | copy-start | bytes 4732
  62.6 3.5 copy-start.47
  73.4 5.3 %copy-start.16 = (bf16[394,768]{1,0:T(8,128)(2,1)S(1)}, bf16[394,768]{1,0:T(8,128)(2,1)}, u32[]{:S(2)}) copy-start(bf16[394,768]{1,0:T(8,128)(2,1)} %slice.482) | copy-start | bytes 1815556
  78.8 8.2 %copy-start.10 = (bf16[2,197,12,64]{1,3,2,0:T(8,128)(2,1)}, bf16[2,197,12,64]{1,3,2,0:T(8,128)(2,1)S(1)}, u32[]{:S(2)}) copy-start(bf16[2,197,12,64]{1,3,2,0:T(8,128)(2,1)S(1)} %copy.56) | copy-start | bytes 1815556
  83.1 3.9 copy-start.9
  95.2 168.1 %copy-start.5 = (f32[394,768]{1,0:T(8,128)}, f32[394,768]{1,0:T(8,128)S(1)}, u32[]{:S(2)}) copy-start(f32[394,768]{1,0:T(8,128)S(1)} %get-tuple-element.167) | copy-start | bytes 3631108
  96.6 2.7 copy-start.17
  96.8 5.0 %copy-start.49 = (f32[394]{0:T(512)}, f32[394]{0:T(512)S(1)}, u32[]{:S(2)}) copy-start(f32[394]{0:T(512)S(1)} %get-tuple-element.80) | copy-start | bytes 4732
  96.8 5.0 %copy-start.51 = (f32[394]{0:T(512)}, f32[394]{0:T(512)S(1)}, u32[]{:S(2)}) copy-start(f32[394]{0:T(512)S(1)} %get-tuple-element.81) | copy-start | bytes 4732
  167.5 7.6 %copy-start.21 = (bf16[1,4,4,96,768]{4,3,2,1,0:T(8,128)(2,1)S(1)}, bf16[1,4,4,96,768]{4,3,2,1,0:T(8,128)(2,1)}, u32[]{:S(2)}) copy-start(bf16[1,4,4,96,768]{4,3,2,1,0:T(8,128)(2,1)} %get-tuple-element.97) | copy-start | bytes 7077892
  167.5 7.6 %copy-start.44 = (bf16[4,256,768]{2,1,0:T(8,128)(2,1)S(1)}, bf16[4,256,768]{2,1,0:T(8,128)(2,1)}, u32[]{:S(2)}) copy-start(bf16[4,256,768]{2,1,0:T(8,128)(2,1)} %get-tuple-element.27) | copy-start | bytes 4718596
  179.7 7.0 %copy-start.23 = (bf16[1,4,4,96,768]{4,3,2,1,0:T(8,128)(2,1)S(1)}, bf16[1,4,4,96,768]{4,3,2,1,0:T(8,128)(2,1)}, u32[]{:S(2)}) copy-start(bf16[1,4,4,96,768]{4,3,2,1,0:T(8,128)(2,1)} %get-tuple-element.98) | copy-start | bytes 7077892
  179.7 7.0 %copy-start.46 = (f32[1024,1536]{1,0:T(8,128)S(1)}, f32[1024,1536]{1,0:T(8,128)}, u32[]{:S(2)}) copy-start(f32[1024,1536]{1,0:T(8,128)} %fusion.176) | copy-start | bytes 18874372
  191.0 3.8 copy-start.26
  192.1 45.4 %collective-permute-start.2 = (bf16[256,768]{1,0:T(8,128)(2,1)}, bf16[256,768]{1,0:T(8,128)(2,1)}, u32[]{:S(2)}, u32[]{:S(2)}) collective-permute-start(bf16[256,768]{1,0:T(8,128)(2,1)} %get-tuple-element.115), channel_id=1, source_target_pairs={{0,6},{1,7},{2,4},{3,5},{4,2},{5,3},{6,0},{7,1},{8,14},{9,15},{10,... | collective-permute-start | bytes 1179656 | tf_op jit(solution)/shard_map/ppermute | solution.py:50
  192.1 46.4 %collective-permute-start.1 = (bf16[256,768]{1,0:T(8,128)(2,1)}, bf16[256,768]{1,0:T(8,128)(2,1)}, u32[]{:S(2)}, u32[]{:S(2)}) collective-permute-start(bf16[256,768]{1,0:T(8,128)(2,1)} %get-tuple-element.116), channel_id=1, source_target_pairs={{0,4},{1,5},{2,6},{3,7},{4,0},{5,1},{6,2},{7,3},{8,12},{9,13},{10,... | collective-permute-start | bytes 1179656 | tf_op jit(solution)/shard_map/ppermute | solution.py:50
  192.1 50.2 %collective-permute-start = (bf16[256,768]{1,0:T(8,128)(2,1)}, bf16[256,768]{1,0:T(8,128)(2,1)}, u32[]{:S(2)}, u32[]{:S(2)}) collective-permute-start(bf16[256,768]{1,0:T(8,128)(2,1)} %get-tuple-element.117), channel_id=1, source_target_pairs={{0,2},{1,3},{2,0},{3,1},{4,6},{5,7},{6,4},{7,5},{8,10},{9,11},{10,... | collective-permute-start | bytes 1179656 | tf_op jit(solution)/shard_map/ppermute | solution.py:50
  194.8 19.0 %slice-start.4 = ((s8[6291456]{0:T(1024)(128)(4,1)}), s8[4194304]{0:T(1024)(128)(4,1)S(1)}, s32[]{:S(2)}) async-start(s8[6291456]{0:T(1024)(128)(4,1)} %bitcast.201), calls=%async_computation.4 | async-start | bytes 8388608
  198.8 6.9 %copy-start.45 = (bf16[4,256,768]{2,1,0:T(8,128)(2,1)S(1)}, bf16[4,256,768]{2,1,0:T(8,128)(2,1)}, u32[]{:S(2)}) copy-start(bf16[4,256,768]{2,1,0:T(8,128)(2,1)} %get-tuple-element.27) | copy-start | bytes 4718596
  198.8 15.0 %slice-start.5 = ((s8[6291456]{0:T(1024)(128)(4,1)}), s8[2097152]{0:T(1024)(128)(4,1)S(1)}, s32[]{:S(2)}) async-start(s8[6291456]{0:T(1024)(128)(4,1)} %bitcast.201), calls=%async_computation.5 | async-start | bytes 4194304
  208.6 5.2 %copy-start.20 = (bf16[1,4,4,96,768]{4,3,2,1,0:T(8,128)(2,1)S(1)}, bf16[1,4,4,96,768]{4,3,2,1,0:T(8,128)(2,1)}, u32[]{:S(2)}) copy-start(bf16[1,4,4,96,768]{4,3,2,1,0:T(8,128)(2,1)} %get-tuple-element.100) | copy-start | bytes 7077892
  211.3 9.8 %copy-start.19 = (bf16[1,4,4,96,768]{4,3,2,1,0:T(8,128)(2,1)S(1)}, bf16[1,4,4,96,768]{4,3,2,1,0:T(8,128)(2,1)}, u32[]{:S(2)}) copy-start(bf16[1,4,4,96,768]{4,3,2,1,0:T(8,128)(2,1)} %get-tuple-element.99) | copy-start | bytes 7077892
  211.3 40.8 %collective-permute-start.3 = (bf16[2,1536,768]{2,1,0:T(8,128)(2,1)}, bf16[2,1536,768]{2,1,0:T(8,128)(2,1)}, u32[]{:S(2)}, u32[]{:S(2)}) collective-permute-start(bf16[2,1536,768]{2,1,0:T(8,128)(2,1)} %pad_maximum_fusion.1), channel_id=1, source_target_pairs={{0,1},{1,0},{2,3},{3,2},{4,5},{5,4},{6,7},{7,6},{8,9},{9,8},{10,11... | collective-permute-start | bytes 14155784 | tf_op jit(solution)/shard_map/ppermute | solution.py:54
  227.4 16.4 %collective-permute-start.6 = (bf16[256,768]{1,0:T(8,128)(2,1)}, bf16[256,768]{1,0:T(8,128)(2,1)}, u32[]{:S(2)}, u32[]{:S(2)}) collective-permute-start(bf16[256,768]{1,0:T(8,128)(2,1)} %get-tuple-element.111), channel_id=1, source_target_pairs={{0,6},{1,7},{2,4},{3,5},{4,2},{5,3},{6,0},{7,1},{8,14},{9,15},{10,... | collective-permute-start | bytes 1179656 | tf_op jit(solution)/shard_map/ppermute | solution.py:50
  237.6 11.1 %collective-permute-start.5 = (bf16[256,768]{1,0:T(8,128)(2,1)}, bf16[256,768]{1,0:T(8,128)(2,1)}, u32[]{:S(2)}, u32[]{:S(2)}) collective-permute-start(bf16[256,768]{1,0:T(8,128)(2,1)} %get-tuple-element.112), channel_id=1, source_target_pairs={{0,4},{1,5},{2,6},{3,7},{4,0},{5,1},{6,2},{7,3},{8,12},{9,13},{10,... | collective-permute-start | bytes 1179656 | tf_op jit(solution)/shard_map/ppermute | solution.py:50
  238.5 11.0 %collective-permute-start.4 = (bf16[256,768]{1,0:T(8,128)(2,1)}, bf16[256,768]{1,0:T(8,128)(2,1)}, u32[]{:S(2)}, u32[]{:S(2)}) collective-permute-start(bf16[256,768]{1,0:T(8,128)(2,1)} %get-tuple-element.113), channel_id=1, source_target_pairs={{0,2},{1,3},{2,0},{3,1},{4,6},{5,7},{6,4},{7,5},{8,10},{9,11},{10,... | collective-permute-start | bytes 1179656 | tf_op jit(solution)/shard_map/ppermute | solution.py:50
  242.3 7.2 %copy-start.24 = (bf16[256,768]{1,0:T(8,128)(2,1)S(1)}, bf16[256,768]{1,0:T(8,128)(2,1)}, u32[]{:S(2)}) copy-start(bf16[256,768]{1,0:T(8,128)(2,1)} %get-tuple-element.110) | copy-start | bytes 1179652
  243.9 16.1 %copy-start.25 = (bf16[1024,768]{1,0:T(8,128)(2,1)}, bf16[1024,768]{1,0:T(8,128)(2,1)S(1)}, u32[]{:S(2)}) copy-start(bf16[1024,768]{1,0:T(8,128)(2,1)S(1)} %pad_maximum_fusion.3) | copy-start | bytes 4718596
  258.2 2.9 copy-start.1
  273.8 31.7 %collective-permute-start.7 = (bf16[2,384,768]{2,1,0:T(8,128)(2,1)}, bf16[2,384,768]{2,1,0:T(8,128)(2,1)}, u32[]{:S(2)}, u32[]{:S(2)}) collective-permute-start(bf16[2,384,768]{2,1,0:T(8,128)(2,1)} %get-tuple-element.96), channel_id=1, source_target_pairs={{0,8},{1,9},{2,10},{3,11},{4,12},{5,13},{6,14},{7,15}} | collective-permute-start | bytes 3538952 | tf_op jit(solution)/shard_map/ppermute | solution.py:61
  275.1 30.4 %collective-permute-start.8 = (bf16[2,384,768]{2,1,0:T(8,128)(2,1)}, bf16[2,384,768]{2,1,0:T(8,128)(2,1)}, u32[]{:S(2)}, u32[]{:S(2)}) collective-permute-start(bf16[2,384,768]{2,1,0:T(8,128)(2,1)} %get-tuple-element.95), channel_id=1, source_target_pairs={{24,16},{25,17},{26,18},{27,19},{28,20},{29,21},{30,22},{31,23}} | collective-permute-start | bytes 3538952 | tf_op jit(solution)/shard_map/ppermute | solution.py:61
  282.6 3.9 copy-start.15
  305.5 18.8 %slice-start = ((s8[4915200]{0:T(1024)(128)(4,1)}), s8[720896]{0:T(1024)(128)(4,1)S(1)}, s32[]{:S(2)}) async-start(s8[4915200]{0:T(1024)(128)(4,1)} %bitcast.145), calls=%async_computation | async-start | bytes 1441792
  311.6 12.7 %slice-start.1 = ((s8[4915200]{0:T(1024)(128)(4,1)}), s8[4194304]{0:T(1024)(128)(4,1)S(1)}, s32[]{:S(2)}) async-start(s8[4915200]{0:T(1024)(128)(4,1)} %bitcast.145), calls=%async_computation.1 | async-start | bytes 8388608
  316.3 8.0 %copy-start = (f32[2,12,197,197]{2,3,1,0:T(8,128)S(1)}, f32[2,12,197,197]{2,3,1,0:T(8,128)}, u32[]{:S(2)}) copy-start(f32[2,12,197,197]{2,3,1,0:T(8,128)} %copy.65) | copy-start | bytes 11176996
  320.5 27.9 %collective-permute-start.9 = (bf16[2,384,768]{2,1,0:T(8,128)(2,1)}, bf16[2,384,768]{2,1,0:T(8,128)(2,1)}, u32[]{:S(2)}, u32[]{:S(2)}) collective-permute-start(bf16[2,384,768]{2,1,0:T(8,128)(2,1)} %get-tuple-element.94), channel_id=1, source_target_pairs={{0,8},{1,9},{2,10},{3,11},{4,12},{5,13},{6,14},{7,15},{8,16},{9,17... | collective-permute-start | bytes 3538952 | tf_op jit(solution)/shard_map/ppermute | solution.py:61
  322.8 27.4 %collective-permute-start.10 = (bf16[2,384,768]{2,1,0:T(8,128)(2,1)}, bf16[2,384,768]{2,1,0:T(8,128)(2,1)}, u32[]{:S(2)}, u32[]{:S(2)}) collective-permute-start(bf16[2,384,768]{2,1,0:T(8,128)(2,1)} %get-tuple-element.93), channel_id=1, source_target_pairs={{16,8},{17,9},{18,10},{19,11},{20,12},{21,13},{22,14},{23,15},{24,... | collective-permute-start | bytes 3538952 | tf_op jit(solution)/shard_map/ppermute | solution.py:61
  334.5 19.8 %copy-start.48 = (bf16[394,768]{1,0:T(8,128)(2,1)S(1)}, bf16[394,768]{1,0:T(8,128)(2,1)}, u32[]{:S(2)}) copy-start(bf16[394,768]{1,0:T(8,128)(2,1)} %copy-done.47) | copy-start | bytes 1815556
  362.0 9.8 %copy-start.12 = (bf16[768,2304]{1,0:T(8,128)(2,1)S(1)}, bf16[768,2304]{1,0:T(8,128)(2,1)}, u32[]{:S(2)}) copy-start(bf16[768,2304]{1,0:T(8,128)(2,1)} %convolution_convert_fusion) | copy-start | bytes 10616836
  362.0 9.8 %copy-start.28 = (bf16[768,768]{1,0:T(8,128)(2,1)S(1)}, bf16[768,768]{1,0:T(8,128)(2,1)}, u32[]{:S(2)}) copy-start(bf16[768,768]{1,0:T(8,128)(2,1)} %convolution_convert_fusion.7) | copy-start | bytes 3538948
  366.5 26.4 %collective-permute-start.19 = (bf16[2,384,768]{2,1,0:T(8,128)(2,1)}, bf16[2,384,768]{2,1,0:T(8,128)(2,1)}, u32[]{:S(2)}, u32[]{:S(2)}) collective-permute-start(bf16[2,384,768]{2,1,0:T(8,128)(2,1)} %get-tuple-element.92), channel_id=1, source_target_pairs={{8,0},{9,1},{10,2},{11,3},{12,4},{13,5},{14,6},{15,7},{16,8},{17,9... | collective-permute-start | bytes 3538952 | tf_op jit(solution)/shard_map/ppermute | solution.py:61
  368.4 26.4 %collective-permute-start.18 = (bf16[2,384,768]{2,1,0:T(8,128)(2,1)}, bf16[2,384,768]{2,1,0:T(8,128)(2,1)}, u32[]{:S(2)}, u32[]{:S(2)}) collective-permute-start(bf16[2,384,768]{2,1,0:T(8,128)(2,1)} %get-tuple-element.91), channel_id=1, source_target_pairs={{0,8},{1,9},{2,10},{3,11},{4,12},{5,13},{6,14},{7,15},{8,16},{9,17... | collective-permute-start | bytes 3538952 | tf_op jit(solution)/shard_map/ppermute | solution.py:61
  372.5 2.9 copy-start.2
  372.5 6.8 %copy-start.6 = (f32[394,768]{1,0:T(8,128)S(1)}, f32[394,768]{1,0:T(8,128)}, u32[]{:S(2)}) copy-start(f32[394,768]{1,0:T(8,128)} %copy-done.5) | copy-start | bytes 3631108
  372.5 6.8 %copy-start.50 = (f32[394]{0:T(512)S(1)}, f32[394]{0:T(512)}, u32[]{:S(2)}) copy-start(f32[394]{0:T(512)} %copy-done.49) | copy-start | bytes 4732
  372.5 6.8 %copy-start.52 = (f32[394]{0:T(512)S(1)}, f32[394]{0:T(512)}, u32[]{:S(2)}) copy-start(f32[394]{0:T(512)} %copy-done.51) | copy-start | bytes 4732
  375.4 36.3 %collective-permute-start.11 = (bf16[384,3200]{1,0:T(8,128)(2,1)}, bf16[384,3200]{1,0:T(8,128)(2,1)}, u32[]{:S(2)}, u32[]{:S(2)}) collective-permute-start(bf16[384,3200]{1,0:T(8,128)(2,1)} %slice.382), channel_id=1, source_target_pairs={{0,1},{1,0},{2,3},{3,2},{4,5},{5,4},{6,7},{7,6},{8,9},{9,8},{10,11... | collective-permute-start | bytes 7372808 | tf_op jit(solution)/shard_map/ppermute | solution.py:54
  382.6 17.4 %copy-start.8 = (f32[394,768]{1,0:T(8,128)S(1)}, f32[394,768]{1,0:T(8,128)}, u32[]{:S(2)}) copy-start(f32[394,768]{1,0:T(8,128)} %copy-done.7) | copy-start | bytes 3631108
  382.6 17.4 %copy-start.18 = (bf16[394,768]{1,0:T(8,128)(2,1)S(1)}, bf16[394,768]{1,0:T(8,128)(2,1)}, u32[]{:S(2)}) copy-start(bf16[394,768]{1,0:T(8,128)(2,1)} %param.31) | copy-start | bytes 1815556
  397.2 14.6 %slice-start.2 = ((s8[4915200]{0:T(1024)(128)(4,1)}), s8[4194304]{0:T(1024)(128)(4,1)S(1)}, s32[]{:S(2)}) async-start(s8[4915200]{0:T(1024)(128)(4,1)} %bitcast.147), calls=%async_computation.2 | async-start | bytes 8388608
  397.3 6.6 %collective-permute-start.20 = (bf16[2,96,768]{2,1,0:T(8,128)(2,1)S(1)}, bf16[2,96,768]{2,1,0:T(8,128)(2,1)S(1)}, u32[]{:S(2)}, u32[]{:S(2)}) collective-permute-start(bf16[2,96,768]{2,1,0:T(8,128)(2,1)S(1)} %get-tuple-element.120), channel_id=1, source_target_pairs={{0,6},{1,7},{2,4},{3,5},{4,2},{5,3},{6,0},{7,1},{8,14},{9,15},{10,... | collective-permute-start | bytes 884744 | tf_op jit(solution)/shard_map/ppermute | solution.py:50
  398.8 12.8 %collective-permute-start.21 = (bf16[2,96,768]{2,1,0:T(8,128)(2,1)S(1)}, bf16[2,96,768]{2,1,0:T(8,128)(2,1)S(1)}, u32[]{:S(2)}, u32[]{:S(2)}) collective-permute-start(bf16[2,96,768]{2,1,0:T(8,128)(2,1)S(1)} %get-tuple-element.119), channel_id=1, source_target_pairs={{0,4},{1,5},{2,6},{3,7},{4,0},{5,1},{6,2},{7,3},{8,12},{9,13},{10,... | collective-permute-start | bytes 884744 | tf_op jit(solution)/shard_map/ppermute | solution.py:50
  399.7 12.0 %slice-start.3 = ((s8[4915200]{0:T(1024)(128)(4,1)}), s8[720896]{0:T(1024)(128)(4,1)S(1)}, s32[]{:S(2)}) async-start(s8[4915200]{0:T(1024)(128)(4,1)} %bitcast.147), calls=%async_computation.3 | async-start | bytes 1441792
  399.7 11.9 %collective-permute-start.22 = (bf16[2,96,768]{2,1,0:T(8,128)(2,1)S(1)}, bf16[2,96,768]{2,1,0:T(8,128)(2,1)S(1)}, u32[]{:S(2)}, u32[]{:S(2)}) collective-permute-start(bf16[2,96,768]{2,1,0:T(8,128)(2,1)S(1)} %get-tuple-element.118), channel_id=1, source_target_pairs={{0,2},{1,3},{2,0},{3,1},{4,6},{5,7},{6,4},{7,5},{8,10},{9,11},{10,... | collective-permute-start | bytes 884744 | tf_op jit(solution)/shard_map/ppermute | solution.py:50
  414.3 14.0 %collective-permute-start.14 = (bf16[96,3200]{1,0:T(8,128)(2,1)S(1)}, bf16[96,3200]{1,0:T(8,128)(2,1)S(1)}, u32[]{:S(2)}, u32[]{:S(2)}) collective-permute-start(bf16[96,3200]{1,0:T(8,128)(2,1)S(1)} %get-tuple-element.104), channel_id=1, source_target_pairs={{0,6},{1,7},{2,4},{3,5},{4,2},{5,3},{6,0},{7,1},{8,14},{9,15},{10,... | collective-permute-start | bytes 1843208 | tf_op jit(solution)/shard_map/ppermute | solution.py:50
  416.1 28.1 %collective-permute-start.13 = (bf16[96,3200]{1,0:T(8,128)(2,1)S(1)}, bf16[96,3200]{1,0:T(8,128)(2,1)S(1)}, u32[]{:S(2)}, u32[]{:S(2)}) collective-permute-start(bf16[96,3200]{1,0:T(8,128)(2,1)S(1)} %get-tuple-element.105), channel_id=1, source_target_pairs={{0,4},{1,5},{2,6},{3,7},{4,0},{5,1},{6,2},{7,3},{8,12},{9,13},{10,... | collective-permute-start | bytes 1843208 | tf_op jit(solution)/shard_map/ppermute | solution.py:50
  416.6 27.6 %collective-permute-start.12 = (bf16[96,3200]{1,0:T(8,128)(2,1)S(1)}, bf16[96,3200]{1,0:T(8,128)(2,1)S(1)}, u32[]{:S(2)}, u32[]{:S(2)}) collective-permute-start(bf16[96,3200]{1,0:T(8,128)(2,1)S(1)} %get-tuple-element.103), channel_id=1, source_target_pairs={{0,2},{1,3},{2,0},{3,1},{4,6},{5,7},{6,4},{7,5},{8,10},{9,11},{10,... | collective-permute-start | bytes 1843208 | tf_op jit(solution)/shard_map/ppermute | solution.py:50
  444.5 7.2 %collective-permute-start.17 = (bf16[24,3200]{1,0:T(8,128)(2,1)S(1)}, bf16[24,3200]{1,0:T(8,128)(2,1)S(1)}, u32[]{:S(2)}, u32[]{:S(2)}) collective-permute-start(bf16[24,3200]{1,0:T(8,128)(2,1)S(1)} %get-tuple-element.124), channel_id=1, source_target_pairs={{0,8},{1,9},{2,10},{3,11},{4,12},{5,13},{6,14},{7,15},{8,16},{9,17... | collective-permute-start | bytes 460808 | tf_op jit(solution)/shard_map/ppermute | solution.py:65
  445.5 12.7 %collective-permute-start.16 = (bf16[24,3200]{1,0:T(8,128)(2,1)S(1)}, bf16[24,3200]{1,0:T(8,128)(2,1)S(1)}, u32[]{:S(2)}, u32[]{:S(2)}) collective-permute-start(bf16[24,3200]{1,0:T(8,128)(2,1)S(1)} %get-tuple-element.125), channel_id=1, source_target_pairs={{0,16},{1,17},{2,18},{3,19},{4,20},{5,21},{6,22},{7,23},{8,24},{9,... | collective-permute-start | bytes 460808 | tf_op jit(solution)/shard_map/ppermute | solution.py:65
  446.6 14.2 %collective-permute-start.15 = (bf16[24,3200]{1,0:T(8,128)(2,1)S(1)}, bf16[24,3200]{1,0:T(8,128)(2,1)S(1)}, u32[]{:S(2)}, u32[]{:S(2)}) collective-permute-start(bf16[24,3200]{1,0:T(8,128)(2,1)S(1)} %get-tuple-element.123), channel_id=1, source_target_pairs={{0,24},{1,25},{2,26},{3,27},{4,28},{5,29},{6,30},{7,31},{8,0},{9,1... | collective-permute-start | bytes 460808 | tf_op jit(solution)/shard_map/ppermute | solution.py:65
  (18 other events, 30.9 us)
where the time goes:
time: 475 us; the launch traced here: 466 us
  matrix products  113 us (24%)
  Pallas kernels  103 us (22%)
  waiting for transfers between devices  95.7 us (20%)
  local copies, waits for them, and re-layouts  74.9 us (16%)
  other arithmetic  44.2 us (9%)
  starting transfers between devices  32.6 us (7%)
    dot_general x28, matrix products, dot_f32(): lax.dot_general(left, right, (((left_dim,), (right_dim,)), ((), ())), pre...  85.2 us
    pallas_call x1, Pallas kernels, exchange_rows(): pl.pallas_call(functools.partial(exchange_kernel, planes), out_shape=(lik...  55.2 us
    pallas_call x1, Pallas kernels, gather_weights(): pl.pallas_call(functools.partial(gather_kernel, planes), out_shape=(jax.S...  48 us
    ppermute x6, waiting for transfers between devices, along_line(): return lax.ppermute(array, 'fsdp', pairs)  43.8 us
    ppermute x12, waiting for transfers between devices, to_chip(): return lax.ppermute(array, 'fsdp', [(i, i ^ 2 * k) for i in range(n_dev)])  42.7 us
    ppermute x6, starting transfers between devices, along_line(): return lax.ppermute(array, 'fsdp', pairs)  12.1 us
    ppermute x12, starting transfers between devices, to_chip(): return lax.ppermute(array, 'fsdp', [(i, i ^ 2 * k) for i in range(n_dev)])  10.8 us
    slice x2, local copies, waits for them, and re-layouts, on_device(): w_in = [half[0] for half in halves]  9.71 us
  transfers between devices with their start and end apart: 23, of which 13 were waited for; matrix products, arithmetic and copies ran while one was open for 18% of the time, Pallas kernels for 0%

commit v1 on v0

--- a/solution.py
+++ b/solution.py
@@ -7,7 +7,6 @@
 from jax.experimental.pallas import tpu as pltpu
 from jax.sharding import PartitionSpec as P
 
-HEADS = 12
 HD = 64
 EXPERTS = 4
 TOP = 2
@@ -16,13 +15,6 @@
 SLOTS = 256
 PLANE = 2 * EXPERTS
 LANES = 128
-
-
-def layer_norm(values, gain_vec, shift_vec):
-    row_mean = jnp.mean(values, axis=-1, keepdims=True)
-    centred = values - row_mean
-    spread = jnp.mean(centred * centred, axis=-1, keepdims=True)
-    return centred * lax.rsqrt(spread + 1e-06) * gain_vec + shift_vec
 
 
 def gelu_tanh(values):
@@ -442,6 +434,150 @@
     return slots[0].astype(jnp.float32) + up.astype(jnp.float32) + down.astype(jnp.float32)
 
 
+def row_norm(values):
+    centred = values - jnp.mean(values, axis=-1, keepdims=True)
+    spread = jnp.mean(centred * centred, axis=-1, keepdims=True)
+    return centred, lax.rsqrt(spread + 1e-06)
+
+
+def norm_back(centred, scale, gain_vec, grad):
+    inner = grad * gain_vec
+    unit = centred * scale
+    shared = jnp.mean(inner, axis=-1, keepdims=True)
+    slope = jnp.mean(inner * unit, axis=-1, keepdims=True)
+    return scale * (inner - shared - unit * slope), unit * grad
+
+
+def head_lanes(h):
+    lane = lax.broadcasted_iota(jnp.int32, (1, 2 * HD), 1)
+    return (lane // HD == h).astype(jnp.float32)
+
+
+def head_probs(queries, key_rows):
+    scores = dot_f32(queries, key_rows, 1, 1)
+    key = lax.broadcasted_iota(jnp.int32, scores.shape, 1)
+    scores = jnp.where(key < LEN, scores, -1e30)
+    scores = jnp.exp(scores - jnp.max(scores, axis=-1, keepdims=True))
+    return scores * (1.0 / jnp.sum(scores, axis=-1, keepdims=True))
+
+
+def forward_kernel(
+    tokens, dense, vecs, sort, router, middle, normed2, logits, qkv, normed, attended, heads
+):
+    f32, low = jnp.float32, jnp.bfloat16
+    width = tokens.shape[1]
+    rows = tokens.shape[0] // SEQ_DEV
+    inputs = tokens[...].astype(f32)
+    centred, scale = row_norm(inputs)
+    plain = (centred * scale * vecs[0:1] + vecs[1:2]).astype(low)
+    normed[...] = dot_f32(plain, sort[...], 1, 0).astype(low)
+    queries = dot_f32(normed[...], dense[:, :width], 1, 0)
+    qkv[:, :width] = ((queries + vecs[2:3]) * HD ** (-0.5)).astype(low)
+    key_rows = dot_f32(normed[...], dense[:, width : 2 * width], 1, 0)
+    qkv[:, width : 2 * width] = key_rows.astype(low)
+    values = dot_f32(normed[...], dense[:, 2 * width : 3 * width], 1, 0)
+    qkv[:, 2 * width : 3 * width] = (values + vecs[3:4]).astype(low)
+
+    @pl.loop(0, width // (2 * HD))
+    def _(pair):
+        q_at, k_at, v_at = [
+            pl.ds(pl.multiple_of(pair * 2 * HD + n * width, 2 * HD), 2 * HD) for n in range(3)
+        ]
+        for seq in range(SEQ_DEV):
+            at = pl.ds(seq * rows, rows)
+            total = 0.0
+            for h in range(2):
+                lanes = head_lanes(h)
+                probs = head_probs(qkv[at, q_at] * lanes.astype(low), qkv[at, k_at])
+                total = total + dot_f32(probs.astype(low), qkv[at, v_at], 1, 0) * lanes
+            heads[at, q_at] = total.astype(low)
+
+    attended[...] = dot_f32(heads[...], sort[...], 1, 0).astype(low)
+    branch = dot_f32(attended[...], dense[:, 3 * width : 4 * width], 1, 0)
+    middle[...] = inputs + branch + vecs[4:5]
+    centred, scale = row_norm(middle[...])
+    normed2[...] = (centred * scale * vecs[5:6] + vecs[6:7]).astype(low)
+    logits[...] = dot_f32(normed2[...], router[...], 1, 1)
+
+
+def backward_kernel(
+    tokens, dense, vecs, sort, middle, qkv, normed, attended, out_grad, grad_normed2,
+    dense_grad, tokens_grad, sums, grad_mid, heads, grads,
+):
+    f32, low = jnp.float32, jnp.bfloat16
+    width = tokens.shape[1]
+    rows = tokens.shape[0] // SEQ_DEV
+
+    def total(rows_of):
+        return jnp.sum(rows_of, axis=0, keepdims=True)
+
+    centred, scale = row_norm(middle[...])
+    grad = grad_normed2[...]
+    back, gain_terms = norm_back(centred, scale, vecs[5:6], grad)
+    sums[5:6] = total(gain_terms)
+    sums[6:7] = total(grad)
+    sums[7:8] = jnp.zeros((1, width), f32)
+    grad_mid[...] = out_grad[...].astype(f32) + back
+    branch = grad_mid[...].astype(low)
+    sums[4:5] = total(branch.astype(f32))
+    dense_grad[:, 3 * width : 4 * width] = dot_f32(attended[...], branch, 0, 0).astype(low)
+    grad_att = dot_f32(branch, dense[:, 3 * width : 4 * width], 1, 1).astype(low)
+    heads[...] = dot_f32(grad_att, sort[...], 1, 1).astype(low)
+
+    @pl.loop(0, width // (2 * HD))
+    def _(pair):
+        q_at, k_at, v_at = [
+            pl.ds(pl.multiple_of(pair * 2 * HD + n * width, 2 * HD), 2 * HD) for n in range(3)
+        ]
+        for seq in range(SEQ_DEV):
+            at = pl.ds(seq * rows, rows)
+            queries, key_rows, values = qkv[at, q_at], qkv[at, k_at], qkv[at, v_at]
+            grad_out = heads[at, q_at]
+            grad_q, grad_k, grad_v = 0.0, 0.0, 0.0
+            for h in range(2):
+                lanes = head_lanes(h)
+                probs = head_probs(queries * lanes.astype(low), key_rows)
+                grad_probs = dot_f32(grad_out * lanes.astype(low), values, 1, 1)
+                grad_v = grad_v + dot_f32(probs.astype(low), grad_out, 0, 0) * lanes
+                shared = jnp.sum(probs * grad_probs, axis=-1, keepdims=True)
+                scores = (probs * (grad_probs - shared)).astype(low)
+                grad_q = grad_q + dot_f32(scores, key_rows, 1, 0) * lanes
+                grad_k = grad_k + dot_f32(scores, queries, 0, 0) * lanes
+            grads[at, q_at] = (grad_q.astype(low).astype(f32) * HD ** (-0.5)).astype(low)
+            grads[at, k_at] = grad_k.astype(low)
+            grads[at, v_at] = grad_v.astype(low)
+
+    sums[2:3] = total(grads[:, :width].astype(f32))
+    sums[3:4] = total(grads[:, 2 * width :].astype(f32))
+    for n in range(3):
+        at = pl.ds(n * width, width)
+        dense_grad[:, at] = dot_f32(normed[...], grads[:, at], 0, 0).astype(low)
+    grad = dot_f32(grads[...], dense[:, : 3 * width], 1, 1)
+    upper = grad.astype(low)
+    lower = (grad - upper.astype(f32)).astype(low)
+    grad = dot_f32(upper, sort[...], 1, 1) + dot_f32(lower, sort[...], 1, 1)
+    centred, scale = row_norm(tokens[...].astype(f32))
+    back, gain_terms = norm_back(centred, scale, vecs[0:1], grad)
+    sums[0:1] = total(gain_terms)
+    sums[1:2] = total(grad)
+    tokens_grad[...] = grad_mid[...] + back
+
+
+def local_call(kernel, outs, scratch, flops, args):
+    spec = pl.BlockSpec(memory_space=pltpu.VMEM)
+    return pl.pallas_call(
+        kernel,
+        out_shape=tuple(jax.ShapeDtypeStruct(shape, kind) for shape, kind in outs),
+        in_specs=[spec] * len(args),
+        out_specs=(spec,) * len(outs),
+        scratch_shapes=[pltpu.VMEM(shape, kind) for shape, kind in scratch],
+        compiler_params=pltpu.CompilerParams(vmem_limit_bytes=48 * 1024 * 1024),
+        cost_estimate=pl.CostEstimate(
+            flops=flops, bytes_accessed=20_000_000, transcendentals=1_000_000
+        ),
+    )(*args)
+
+
 def on_device(
     n_dev,
     tokens,
@@ -464,9 +600,21 @@
     highest = lax.Precision.HIGHEST
     f32 = jnp.float32
     low = jnp.bfloat16
-    row_count, model_width = tokens.shape
-    shape_four = (SEQ_DEV, LEN, HEADS, HD)
-    query_scale = HD ** (-0.5)
+    model_width = tokens.shape[1]
+    spare = -LEN % 16
+    row_count = SEQ_DEV * (LEN + spare)
+
+    def spread_rows(array, fill=0):
+        array = array.reshape(SEQ_DEV, LEN, -1)
+        array = jnp.pad(array, ((0, 0), (0, spare), (0, 0)), constant_values=fill)
+        return array.reshape(row_count, -1)
+
+    def close_rows(array):
+        return array.reshape(SEQ_DEV, LEN + spare, -1)[:, :LEN].reshape(SEQ_DEV * LEN, -1)
+
+    tokens = spread_rows(tokens)
+    out_grad = spread_rows(out_grad)
+    routes = spread_rows(routes, -1)
     own = qkv_weight.shape[0]
     units = expert_in.shape[0]
     planes = n_dev // PLANE
@@ -514,20 +662,13 @@
     dense, own_half = gather_weights(dense_mine, weight_mine, n_dev)
     dense = dense.reshape(model_width, wide + LANES)
 
-    w_qkv = dense[:, : 3 * model_width]
-    w_proj = dense[:, 3 * model_width : wide]
     small = dense[:, wide:].reshape(n_dev, small_room)
     small = dot_f32(sort_dense, small, 1, 0).astype(low)
     gain1, shift1, bias_qv, bias_proj, gain2, shift2, w_router, bias_out, bias_in = take_columns(
         small, small_widths
     )
-    gain1 = gain1.reshape(-1).astype(f32)
-    shift1 = shift1.reshape(-1).astype(f32)
-    gain2 = gain2.reshape(-1).astype(f32)
-    shift2 = shift2.reshape(-1).astype(f32)
-    bias_proj = bias_proj.reshape(-1).astype(f32)
-    bias_q = bias_qv[:, :own].reshape(-1).astype(f32)
-    bias_v = bias_qv[:, own:].reshape(-1).astype(f32)
+    vecs = [gain1, shift1, bias_qv[:, :own], bias_qv[:, own:], bias_proj, gain2, shift2, shift2]
+    vecs = jnp.stack([v.reshape(-1) for v in vecs]).astype(f32)
     w_router = jnp.stack([p.reshape(-1) for p in take_columns(w_router, [own] * EXPERTS)])
     bias_out = jnp.stack([p.reshape(-1) for p in take_columns(bias_out, [own] * EXPERTS)])
     mine = (jnp.arange(EXPERTS, dtype=jnp.int32) == chip).astype(f32)
@@ -548,25 +689,23 @@
         hit.append(slot_ids == (routes[:, j : j + 1] ^ chip) * SLOTS + slot)
     dispatch = (hit[0] | hit[1]).astype(low)
 
-    inputs = tokens.astype(f32)
-    normed_full, norm1_pull = jax.vjp(layer_norm, inputs, gain1, shift1)
-    normed = dot_f32(normed_full.astype(low), sort_rows, 1, 0).astype(low)
-    projected = jnp.dot(normed, w_qkv, preferred_element_type=f32)
-    queries = ((projected[:, :model_width] + bias_q) * query_scale).astype(low).reshape(shape_four)
-    key_rows = projected[:, model_width : 2 * model_width].astype(low).reshape(shape_four)
-    values = (projected[:, 2 * model_width :] + bias_v).astype(low).reshape(shape_four)
-    scores = jnp.einsum("sqhd,skhd->shqk", queries, key_rows, preferred_element_type=f32)
-    exp_scores = jnp.exp(scores - jnp.max(scores, axis=-1, keepdims=True))
-    probs_full = exp_scores / jnp.sum(exp_scores, axis=-1, keepdims=True)
-    probs_low = probs_full.astype(low)
-    attended = jnp.einsum("shqk,skhd->sqhd", probs_low, values, preferred_element_type=f32)
-    attended = attended.reshape(row_count, model_width).astype(low)
-    attended = dot_f32(attended, sort_rows, 1, 0).astype(low)
-
-    middle = inputs + jnp.dot(attended, w_proj, preferred_element_type=f32) + bias_proj
-    normed2_full, norm2_pull = jax.vjp(layer_norm, middle, gain2, shift2)
-    normed2 = normed2_full.astype(low)
-    gate_probs = jax.nn.softmax(dot_f32(normed2, w_router, 1, 1), axis=-1)
+    square = (row_count, model_width)
+    router = jnp.pad(w_router, ((0, LANES - EXPERTS), (0, 0)))
+    middle, normed2, logits, qkv, normed, attended = local_call(
+        forward_kernel,
+        [
+            (square, f32),
+            (square, low),
+            ((row_count, LANES), f32),
+            ((row_count, 3 * model_width), low),
+            (square, low),
+            (square, low),
+        ],
+        [(square, low)],
+        20_000_000_000,
+        (tokens, dense, vecs, sort_rows, router),
+    )
+    gate_probs = jax.nn.softmax(logits[:, :EXPERTS], axis=-1)
     chosen = [jnp.sum(gate_probs * pick[j], axis=1, keepdims=True) for j in range(TOP)]
     combine = (jnp.where(hit[0], chosen[0], 0.0) + jnp.where(hit[1], chosen[1], 0.0)).astype(low)
 
@@ -627,7 +766,6 @@
 
     block_out = (middle + jnp.dot(combine, result, preferred_element_type=f32)).astype(low)
 
-    grad_top = out_grad.astype(f32)
     slot_dots = dot_f32(out_grad, result, 1, 1)
     grad_gates = sum(
         pick[j] * jnp.sum(jnp.where(hit[j], slot_dots, 0.0), axis=1, keepdims=True)
@@ -639,44 +777,17 @@
     grad_router = jnp.dot(grad_logits.T, normed2.astype(f32), precision=highest)
     grad_normed2 = jnp.dot(grad_logits, w_router.astype(f32), precision=highest)
     grad_normed2 = grad_normed2 + jnp.dot(dispatch, grad_slots, preferred_element_type=f32)
-    grad_mid_norm, grad_gain2, grad_shift2 = norm2_pull(grad_normed2)
-    grad_middle = grad_top + grad_mid_norm
-
-    grad_branch = grad_middle.astype(low)
-    grad_bias_proj = jnp.sum(grad_branch.astype(f32), axis=0)
-    grad_proj = dot_f32(attended, grad_branch, 0, 0)
-    grad_attended = dot_f32(grad_branch, w_proj, 1, 1).astype(low)
-    grad_attended = dot_f32(grad_attended, sort_rows, 1, 1).astype(low).reshape(shape_four)
-    grad_probs = jnp.einsum("sqhd,skhd->shqk", grad_attended, values, preferred_element_type=f32)
-    grad_values = jnp.einsum(
-        "shqk,sqhd->skhd", probs_low, grad_attended, preferred_element_type=f32
-    ).astype(low)
-    grad_probs = after(grad_probs, *hops)
-    hops = scatter_middle(terms, hops, n_dev)
-    grad_scores = (
-        probs_full * (grad_probs - jnp.sum(probs_full * grad_probs, axis=-1, keepdims=True))
-    ).astype(low)
-    grad_queries = jnp.einsum(
-        "shqk,skhd->sqhd", grad_scores, key_rows, preferred_element_type=f32
-    ).astype(low)
-    grad_keys = jnp.einsum(
-        "shqk,sqhd->skhd", grad_scores, queries, preferred_element_type=f32
-    ).astype(low)
-    grad_query_pre = grad_queries.astype(f32).reshape(row_count, model_width) * query_scale
-    grad_values = grad_values.reshape(row_count, model_width)
-    grad_projected = jnp.concatenate(
-        [grad_query_pre.astype(low), grad_keys.reshape(row_count, model_width), grad_values],
-        axis=1,
-    )
-    grad_projected = after(grad_projected, *hops)
-    expert_mine = scatter_end(terms, hops, n_dev).astype(low)
-    grad_qkv = dot_f32(normed, grad_projected, 0, 0)
-    grad_normed = dot_f32(grad_projected, w_qkv, 1, 1)
-    upper = grad_normed.astype(low)
-    lower = (grad_normed - upper.astype(f32)).astype(low)
-    grad_normed = dot_f32(upper, sort_rows, 1, 1) + dot_f32(lower, sort_rows, 1, 1)
-    grad_in_norm, grad_gain1, grad_shift1 = norm1_pull(grad_normed)
-    tokens_grad = grad_middle + grad_in_norm
+    dense_grad, tokens_grad, sums = local_call(
+        backward_kernel,
+        [((model_width, wide), low), (square, f32), ((8, model_width), f32)],
+        [(square, f32), (square, low), ((row_count, 3 * model_width), low)],
+        20_000_000_000,
+        (
+            tokens, dense, vecs, sort_rows, middle, qkv, normed, attended, out_grad,
+            grad_normed2,
+        ),
+    )
+    expert_mine = scatter_end(terms, scatter_middle(terms, hops, n_dev), n_dev).astype(low)
 
     def by_owner(rows):
         return rows.reshape(-1, n_dev, rows.shape[-1] // n_dev).transpose(1, 0, 2).reshape(n_dev, -1)
@@ -686,17 +797,7 @@
             by_owner(
                 jnp.concatenate(
                     [
-                        jnp.stack(
-                            [
-                                grad_gain1,
-                                grad_shift1,
-                                jnp.sum(grad_query_pre, axis=0),
-                                jnp.sum(grad_values.astype(f32), axis=0),
-                                grad_bias_proj,
-                                grad_gain2,
-                                grad_shift2,
-                            ]
-                        ),
+                        sums[:7],
                         grad_router,
                         grad_bias_out,
                     ],
@@ -711,8 +812,7 @@
     small_grads = dot_f32(sort_dense, small_grads, 0, 0).astype(low)
     dense_grads = jnp.concatenate(
         [
-            grad_qkv.astype(low),
-            grad_proj.astype(low),
+            dense_grad,
             small_grads.reshape(n_dev * own, LANES),
         ],
         axis=1,
@@ -736,8 +836,8 @@
     small = dense_out[:, wide:].reshape(1, small_room)
     small = [p[0] for p in take_columns(small, small_widths)]
     return (
-        block_out,
-        tokens_grad,
+        close_rows(block_out),
+        close_rows(tokens_grad),
         small[0],
         small[1],
         dense_out[:, : 3 * model_width],

time: 475 us -> 437 us (0.920)
  the two profiles are of different devices: /device:TPU:9 before, /device:TPU:24 now
where the time goes in v1:
time: 437 us; the launch traced here: 429 us
  Pallas kernels  144 us (33%)
  waiting for transfers between devices  87.7 us (20%)
  matrix products  76.1 us (17%)
  local copies, waits for them, and re-layouts  51.4 us (12%)
  starting transfers between devices  35.6 us (8%)
  other arithmetic  32 us (7%)
    dot_general x19, matrix products, dot_f32(): lax.dot_general(left, right, (((left_dim,), (right_dim,)), ((), ())), pre...  70.8 us
    pallas_call x1, Pallas kernels, exchange_rows(): pl.pallas_call(functools.partial(exchange_kernel, planes), out_shape=(lik...  56.9 us
    pallas_call x1, Pallas kernels, gather_weights(): pl.pallas_call(functools.partial(gather_kernel, planes), out_shape=(jax.S...  48.9 us
    ppermute x6, waiting for transfers between devices, along_line(): return lax.ppermute(array, 'fsdp', pairs)  43.9 us
    pallas_call x2, Pallas kernels, local_call(): pl.pallas_call(kernel, out_shape=tuple((jax.ShapeDtypeStruct(shape, kind)...  38.6 us
    ppermute x3, waiting for transfers between devices, around_line(): lax.ppermute(array, 'fsdp', [(i, (i + shift * PLANE) % n_dev) for i in ra...  29.4 us
    ppermute x6, starting transfers between devices, along_line(): return lax.ppermute(array, 'fsdp', pairs)  15.7 us
    ppermute x12, waiting for transfers between devices, to_chip(): return lax.ppermute(array, 'fsdp', [(i, i ^ 2 * k) for i in range(n_dev)])  14.4 us
  transfers between devices with their start and end apart: 23, of which 8 were waited for; matrix products, arithmetic and copies ran while one was open for 17% of the time, Pallas kernels for 0%

profile of v1, /device:TPU:24, one launch (start us, length us, event | category | flops | bytes accessed | tf_op | source)
XLA Modules:
  0.0 429.0 jit_solution(2628024430355487634)
XLA Ops:
  3.8 3.4 concatenate.31
  7.2 1.4 copy_bitcast_fusion
  10.4 48.9 %shard_map.271 = (bf16[2,4,4,24,3200]{4,3,2,1,0:T(8,128)(2,1)}, bf16[2,4,4,96,768]{4,3,2,1,0:T(8,128)(2,1)}) custom-call(bf16[24,3200]{1,0:T(8,128)(2,1)} %pad_maximum_fusion.4.dense_in, bf16[2,4,96,768]{3,2,1,0:T(8,128)(2,1)} %pad_maximum_fusion.3.weight_in), custom_call_target="tpu_custom_call" | custom-call | bytes 100000000 | tf_op jit(solution)/shard_map/pallas_call | solution.py:272
  62.8 13.3 %shard_map.272 = (f32[416,768]{1,0:T(8,128)S(1)}, bf16[416,768]{1,0:T(8,128)(2,1)S(1)}, f32[416,128]{1,0:T(8,128)S(1)}, bf16[416,2304]{1,0:T(8,128)(2,1)}, bf16[...) custom-call(bf16[416,768]{1,0:T(8,128)(2,1)S(1)} %bitcast.112, bf16[768,3200]{1,0:T(8,128)(2,1)} %bitcast.150, ...), custom_call_target="tpu_custom_call" | custom-call | flops 20000000000 | bytes 20000000 | tf_op jit(solution)/shard_map/pallas_call | solution.py:568
  77.5 2.0 reshape.346
  80.7 2.4 convolution_convert_fusion.5
  83.0 2.5 convolution_convert_fusion.4
  85.5 56.9 %shard_map.273 = (bf16[2,4,4,96,768]{4,3,2,1,0:T(8,128)(2,1)}, bf16[2,4,4,96,768]{4,3,2,1,0:T(8,128)(2,1)}, bf16[4,256,768]{2,1,0:T(8,128)(2,1)}, bf16[4,256,768]{2,1,0:T(8,128)(2,1)}) custom-call(bf16[2,4,4,96,768]{4,3,2,1,0:T(8,128)(2,1)} %get-tuple-element.35.weight_in, bf16[4,256,768]{2,1,0:T(8,128)(2,1)} %bitcast.131, ...), custom_call_target="tpu_custom_call", output_to_operand_aliasing={{0}: (0, {})} | custom-call | bytes 150000000 | tf_op jit(solution)/shard_map/pallas_call | solution.py:389
  142.5 4.9 %fusion.111 = (bf16[1,4,4,96,768]{4,3,2,1,0:T(8,128)(2,1)}, bf16[1,4,4,96,768]{4,3,2,1,0:T(8,128)(2,1)}) fusion(bf16[2,4,4,96,768]{4,3,2,1,0:T(8,128)(2,1)} %get-tuple-element.38), kind=kLoop, calls=%fused_computation.244 | loop fusion | bytes 9437184 | tf_op jit(solution)/shard_map/slice | solution.py:727
  147.7 4.9 %fusion.110 = (bf16[1,4,4,96,768]{4,3,2,1,0:T(8,128)(2,1)}, bf16[1,4,4,96,768]{4,3,2,1,0:T(8,128)(2,1)}) fusion(bf16[2,4,4,96,768]{4,3,2,1,0:T(8,128)(2,1)} %get-tuple-element.39), kind=kLoop, calls=%fused_computation.243 | loop fusion | bytes 9437184 | tf_op jit(solution)/shard_map/slice | solution.py:727
  153.4 7.6 %fusion.120 = f32[1024,1536]{1,0:T(8,128)} fusion(bf16[1024,768]{1,0:T(8,128)(2,1)} %bitcast.165, bf16[1536,768]{1,0:T(8,128)(2,1)} %bitcast.119), kind=kOutput, calls=%fused_computation.253 | convolution fusion | flops 2415919104 | bytes 10223616 | tf_op jit(solution)/shard_map/dot_general | solution.py:33
  160.9 4.5 %fusion.121 = f32[1024,1536]{1,0:T(8,128)} fusion(bf16[1024,768]{1,0:T(8,128)(2,1)S(1)} %bitcast.166, bf16[1536,768]{1,0:T(8,128)(2,1)S(1)} %bitcast.123), kind=kOutput, calls=%fused_computation.254 | convolution fusion | flops 2415919104 | bytes 10223616 | tf_op jit(solution)/shard_map/dot_general | solution.py:33
  165.5 6.9 %fusion.105 = f32[1024,768]{1,0:T(8,128)S(1)} fusion(bf16[1536,768]{1,0:T(8,128)(2,1)} %bitcast.121, f32[1024,1536]{1,0:T(8,128)} %fusion.120, f32[1536]{0:T(1024)S(1)} %add.340), kind=kOutput, calls=%fused_computation.241 | convolution fusion | flops 2431647744 | bytes 11802624 | tf_op jit(solution)/shard_map/dot_general | solution.py:33
  172.6 4.2 add_convert_fusion.2
  176.8 1.2 fusion.114
  178.5 1.5 collective-permute-start.1
  180.0 1.5 collective-permute-start
  181.5 3.9 fusion.16
  185.4 6.8 %convert_reduce_fusion = (f32[1536]{0:T(1024)S(1)}, bf16[1024,1536]{1,0:T(8,128)(2,1)S(1)}) fusion(f32[1024,1536]{1,0:T(8,128)S(1)} %copy-done.30, f32[1536]{0:T(1024)S(1)} %add.345, bf16[1024,768]{1,0:T(8,128)(2,1)S(1)} %bitcast.129, bf16[1536,768]{1,0:T(8,128)(2,1)S(1)} %bitcast.126), kind=kOutput, calls=%fused_computation.20 | convolution fusion | flops 2452093440 | bytes 13381632 | tf_op jit(solution)/shard_map/dot_general | solution.py:33
  192.3 3.0 fusion.15
  195.3 2.5 pad_maximum_fusion
  197.9 7.0 %convert_reduce_fusion.1 = (f32[1536]{0:T(1024)S(1)}, bf16[1024,1536]{1,0:T(8,128)(2,1)S(1)}) fusion(f32[1024,1536]{1,0:T(8,128)S(1)} %bitcast.171, f32[1536]{0:T(1024)S(1)} %add.340, bf16[1024,768]{1,0:T(8,128)(2,1)S(1)} %bitcast.130, bf16[1536,768]{1,0:T(8,128)(2,1)S(1)} %bitcast.122), kind=kOutput, calls=%fused_computation.21 | convolution fusion | flops 2452093440 | bytes 13381632 | tf_op jit(solution)/shard_map/dot_general | solution.py:33
  204.9 2.6 fusion.122
  207.7 2.6 add_convert_fusion.1
  210.3 1.2 fusion.113
  212.1 9.5 %convolution_bitcast_fusion = f32[1,1536,768]{2,1,0:T(8,128)} fusion(bf16[1024,768]{1,0:T(8,128)(2,1)} %bitcast.127, f32[1024,1536]{1,0:T(8,128)} %fusion.120, f32[1536]{0:T(1024)S(1)} %add.340), kind=kOutput, calls=%fused_computation.26 | convolution fusion | flops 2431647744 | bytes 12589056 | tf_op jit(solution)/shard_map/dot_general | solution.py:33
  221.7 4.7 %convolution_bitcast_fusion.1 = f32[1,1536,768]{2,1,0:T(8,128)} fusion(bf16[1024,1536]{1,0:T(8,128)(2,1)S(1)} %copy-done.32, bf16[1024,768]{1,0:T(8,128)(2,1)S(1)} %bitcast.168), kind=kOutput, calls=%fused_computation.27 | convolution fusion | flops 2415919104 | bytes 9437184 | tf_op jit(solution)/shard_map/dot_general | solution.py:33
  226.4 1.6 collective-permute-start.5
  228.0 1.5 collective-permute-start.4
  229.9 2.8 pad_maximum_fusion.1
  232.7 5.3 %collective-permute-done.5 = bf16[256,768]{1,0:T(8,128)(2,1)} collective-permute-done((bf16[256,768]{1,0:T(8,128)(2,1)}, bf16[256,768]{1,0:T(8,128)(2,1)}, u32[]{:S(2)}, u32[]{:S(2)}) %collective-permute-start.5) | collective-permute-done | bytes 393248 | tf_op jit(solution)/shard_map/ppermute | solution.py:42
  238.0 1.2 collective-permute-done.4
  239.2 2.5 pad_maximum_fusion.2
  241.7 7.2 %fusion = bf16[2,1536,768]{2,1,0:T(8,128)(2,1)} fusion(f32[1,1536,768]{2,1,0:T(8,128)S(1)} %copy-done.9, f32[1,1536,768]{2,1,0:T(8,128)} %convolution_bitcast_fusion.1, bf16[2,1536,768]{2,1,0:T(8,128)(2,1)} %collective-permute-done.3), kind=kLoop, calls=%fused_computation.1 | loop fusion | flops 9437184 | bytes 18874368 | tf_op jit(solution)/shard_map/convert_element_type | solution.py:753
  248.9 1.2 select_reduce_fusion.1
  250.6 1.2 fusion.39
  252.5 2.1 convolution_add_fusion.1.grad_normed2
  254.6 25.4 %shard_map.274 = (bf16[768,3072]{1,0:T(8,128)(2,1)}, f32[416,768]{1,0:T(8,128)S(1)}, f32[8,768]{1,0:T(8,128)S(1)}) custom-call(bf16[416,768]{1,0:T(8,128)(2,1)S(1)} %bitcast.113, bf16[768,3200]{1,0:T(8,128)(2,1)} %bitcast.151, f32[8,768]{1,0:T(8,128)S(1)} %convert_element_type.231.vecs, bf16[768,768]{1,0:T(8,128)(2,1)S(1)} %fusion.19.sort, ...), custom_call_target="tpu_custom_call" | custom-call | flops 20000000000 | bytes 20000000 | tf_op jit(solution)/shard_map/pallas_call | solution.py:568
  280.0 4.9 %constant_dynamic-update-slice_fusion.1 = bf16[768,3200]{1,0:T(8,128)(2,1)} fusion(bf16[768,3072]{1,0:T(8,128)(2,1)} %get-tuple-element.47), kind=kLoop, calls=%fused_computation.158 | loop fusion | bytes 9437184
  286.4 2.0 slice.375
  288.5 1.8 fusion.109
  291.1 1.4 collective-permute-start.17
  292.5 26.0 %collective-permute-done.17 = bf16[2,384,768]{2,1,0:T(8,128)(2,1)S(1)} collective-permute-done((bf16[2,384,768]{2,1,0:T(8,128)(2,1)S(1)}, bf16[2,384,768]{2,1,0:T(8,128)(2,1)S(1)}, u32[]{:S(2)}, u32[]{:S(2)}) %collective-permute-start.17) | collective-permute-done | bytes 1179680 | tf_op jit(solution)/shard_map/ppermute | solution.py:53
  318.5 3.2 fusion.17
  322.4 6.0 %collective-permute-start.18 = (bf16[2,384,768]{2,1,0:T(8,128)(2,1)}, bf16[2,384,768]{2,1,0:T(8,128)(2,1)}, u32[]{:S(2)}, u32[]{:S(2)}) collective-permute-start(bf16[2,384,768]{2,1,0:T(8,128)(2,1)} %get-tuple-element.97), channel_id=1, source_target_pairs={{16,8},{17,9},{18,10},{19,11},{20,12},{21,13},{22,14},{23,15},{24,... | collective-permute-start | bytes 3538952 | tf_op jit(solution)/shard_map/ppermute | solution.py:53
  329.0 1.4 copy-done.8
  331.6 1.4 collective-permute-start.10
  333.0 1.5 collective-permute-start.9
  335.1 17.9 %collective-permute-done.18 = bf16[2,384,768]{2,1,0:T(8,128)(2,1)} collective-permute-done((bf16[2,384,768]{2,1,0:T(8,128)(2,1)}, bf16[2,384,768]{2,1,0:T(8,128)(2,1)}, u32[]{:S(2)}, u32[]{:S(2)}) %collective-permute-start.18) | collective-permute-done | bytes 1179680 | tf_op jit(solution)/shard_map/ppermute | solution.py:53
  353.0 3.9 add_convert_fusion.5
  356.9 5.7 %collective-permute-start.19 = (bf16[2,384,768]{2,1,0:T(8,128)(2,1)}, bf16[2,384,768]{2,1,0:T(8,128)(2,1)}, u32[]{:S(2)}, u32[]{:S(2)}) collective-permute-start(bf16[2,384,768]{2,1,0:T(8,128)(2,1)} %get-tuple-element.95), channel_id=1, source_target_pairs={{8,0},{9,1},{10,2},{11,3},{12,4},{13,5},{14,6},{15,7},{16,8},{17,9... | collective-permute-start | bytes 3538952 | tf_op jit(solution)/shard_map/ppermute | solution.py:53
  362.6 1.3 collective-permute-start.16
  363.9 1.9 add_convert_fusion.7
  366.6 3.9 collective-permute-start.13
  370.7 1.6 collective-permute-start.11
  375.6 19.7 %collective-permute-done.13 = bf16[24,3200]{1,0:T(8,128)(2,1)S(1)} collective-permute-done((bf16[24,3200]{1,0:T(8,128)(2,1)}, bf16[24,3200]{1,0:T(8,128)(2,1)S(1)}, u32[]{:S(2)}, u32[]{:S(2)}) %collective-permute-start.13) | collective-permute-done | bytes 153632 | tf_op jit(solution)/shard_map/ppermute | solution.py:57
  395.3 9.7 %collective-permute-done.12 = bf16[24,3200]{1,0:T(8,128)(2,1)} collective-permute-done((bf16[24,3200]{1,0:T(8,128)(2,1)}, bf16[24,3200]{1,0:T(8,128)(2,1)}, u32[]{:S(2)}, u32[]{:S(2)}) %collective-permute-start.12) | collective-permute-done | bytes 153632 | tf_op jit(solution)/shard_map/ppermute | solution.py:57
  408.9 2.4 add_convert_fusion.3
  411.4 1.5 collective-permute-start.20
  412.9 1.8 collective-permute-start.21
  417.0 4.8 %collective-permute-done.20 = bf16[2,96,768]{2,1,0:T(8,128)(2,1)S(1)} collective-permute-done((bf16[2,96,768]{2,1,0:T(8,128)(2,1)S(1)}, bf16[2,96,768]{2,1,0:T(8,128)(2,1)S(1)}, u32[]{:S(2)}, u32[]{:S(2)}) %collective-permute-start.20) | collective-permute-done | bytes 294944 | tf_op jit(solution)/shard_map/ppermute | solution.py:42
  421.8 3.0 collective-permute-done.21
  425.1 1.8 copy.43
  427.0 1.8 copy.44
  (208 shorter events, 31.1 us)
Async XLA Ops:
  0.6 9.1 %copy-start.23 = (bf16[24,768]{1,0:T(8,128)(2,1)S(1)}, bf16[24,768]{1,0:T(8,128)(2,1)}, u32[]{:S(2)}) copy-start(bf16[24,768]{1,0:T(8,128)(2,1)} %param.21) | copy-start | bytes 110596
  0.7 9.1 %copy-start.22 = (bf16[24,2304]{1,0:T(8,128)(2,1)S(1)}, bf16[24,2304]{1,0:T(8,128)(2,1)}, u32[]{:S(2)}) copy-start(bf16[24,2304]{1,0:T(8,128)(2,1)} %param.19) | copy-start | bytes 331780
  0.7 59.6 %copy-start.25 = (s32[32]{0:T(128)}, s32[32]{0:T(128)S(1)}, u32[]{:S(2)}) copy-start(s32[32]{0:T(128)S(1)} %get-tuple-element.167) | copy-start | bytes 388
  8.6 52.1 %copy-start.21 = (bf16[394,768]{1,0:T(8,128)(2,1)S(1)}, bf16[394,768]{1,0:T(8,128)(2,1)}, u32[]{:S(2)}) copy-start(bf16[394,768]{1,0:T(8,128)(2,1)} %param.16) | copy-start | bytes 1815556
  10.4 52.2 %copy-start.24 = (s32[394,2]{0,1:T(2,128)S(1)}, s32[394,2]{0,1:T(2,128)}, u32[]{:S(2)}) copy-start(s32[394,2]{0,1:T(2,128)} %param.30) | copy-start | bytes 9460
  76.0 1.2 copy-start.2
  76.0 1.2 copy-start.4
  76.0 1.4 copy-start.6
  77.2 5.9 %copy-start.33 = (f32[416]{0:T(512)}, f32[416]{0:T(512)S(1)}, u32[]{:S(2)}) copy-start(f32[416]{0:T(512)S(1)} %get-tuple-element.87) | copy-start | bytes 4996
  77.2 5.8 %copy-start.35 = (f32[416]{0:T(512)}, f32[416]{0:T(512)S(1)}, u32[]{:S(2)}) copy-start(f32[416]{0:T(512)S(1)} %get-tuple-element.88) | copy-start | bytes 4996
  80.6 168.3 %copy-start = (bf16[2,208,768]{2,1,0:T(8,128)(2,1)}, bf16[2,208,768]{2,1,0:T(8,128)(2,1)S(1)}, u32[]{:S(2)}) copy-start(bf16[2,208,768]{2,1,0:T(8,128)(2,1)S(1)} %pad.27) | copy-start | bytes 1916932
  147.7 4.9 %copy-start.18 = (bf16[4,256,768]{2,1,0:T(8,128)(2,1)S(1)}, bf16[4,256,768]{2,1,0:T(8,128)(2,1)}, u32[]{:S(2)}) copy-start(bf16[4,256,768]{2,1,0:T(8,128)(2,1)} %get-tuple-element.40) | copy-start | bytes 4718596
  153.3 7.6 %copy-start.12 = (bf16[1,4,4,96,768]{4,3,2,1,0:T(8,128)(2,1)S(1)}, bf16[1,4,4,96,768]{4,3,2,1,0:T(8,128)(2,1)}, u32[]{:S(2)}) copy-start(bf16[1,4,4,96,768]{4,3,2,1,0:T(8,128)(2,1)} %get-tuple-element.100) | copy-start | bytes 7077892
  153.3 7.6 %copy-start.27 = (bf16[4,256,768]{2,1,0:T(8,128)(2,1)S(1)}, bf16[4,256,768]{2,1,0:T(8,128)(2,1)}, u32[]{:S(2)}) copy-start(bf16[4,256,768]{2,1,0:T(8,128)(2,1)} %get-tuple-element.37) | copy-start | bytes 4718596
  165.5 7.0 %copy-start.14 = (bf16[1,4,4,96,768]{4,3,2,1,0:T(8,128)(2,1)S(1)}, bf16[1,4,4,96,768]{4,3,2,1,0:T(8,128)(2,1)}, u32[]{:S(2)}) copy-start(bf16[1,4,4,96,768]{4,3,2,1,0:T(8,128)(2,1)} %get-tuple-element.101) | copy-start | bytes 7077892
  165.5 7.0 %copy-start.30 = (f32[1024,1536]{1,0:T(8,128)S(1)}, f32[1024,1536]{1,0:T(8,128)}, u32[]{:S(2)}) copy-start(f32[1024,1536]{1,0:T(8,128)} %fusion.121) | copy-start | bytes 18874372
  176.8 4.7 %copy-start.19 = (bf16[4,256,768]{2,1,0:T(8,128)(2,1)S(1)}, bf16[4,256,768]{2,1,0:T(8,128)(2,1)}, u32[]{:S(2)}) copy-start(bf16[4,256,768]{2,1,0:T(8,128)(2,1)} %get-tuple-element.40) | copy-start | bytes 4718596
  178.0 48.4 %collective-permute-start.2 = (bf16[256,768]{1,0:T(8,128)(2,1)}, bf16[256,768]{1,0:T(8,128)(2,1)}, u32[]{:S(2)}, u32[]{:S(2)}) collective-permute-start(bf16[256,768]{1,0:T(8,128)(2,1)} %get-tuple-element.116), channel_id=1, source_target_pairs={{0,6},{1,7},{2,4},{3,5},{4,2},{5,3},{6,0},{7,1},{8,14},{9,15},{10,... | collective-permute-start | bytes 1179656 | tf_op jit(solution)/shard_map/ppermute | solution.py:42
  178.5 49.5 %collective-permute-start.1 = (bf16[256,768]{1,0:T(8,128)(2,1)}, bf16[256,768]{1,0:T(8,128)(2,1)}, u32[]{:S(2)}, u32[]{:S(2)}) collective-permute-start(bf16[256,768]{1,0:T(8,128)(2,1)} %get-tuple-element.117), channel_id=1, source_target_pairs={{0,4},{1,5},{2,6},{3,7},{4,0},{5,1},{6,2},{7,3},{8,12},{9,13},{10,... | collective-permute-start | bytes 1179656 | tf_op jit(solution)/shard_map/ppermute | solution.py:42
  180.0 49.9 %collective-permute-start = (bf16[256,768]{1,0:T(8,128)(2,1)}, bf16[256,768]{1,0:T(8,128)(2,1)}, u32[]{:S(2)}, u32[]{:S(2)}) collective-permute-start(bf16[256,768]{1,0:T(8,128)(2,1)} %get-tuple-element.118), channel_id=1, source_target_pairs={{0,2},{1,3},{2,0},{3,1},{4,6},{5,7},{6,4},{7,5},{8,10},{9,11},{10,... | collective-permute-start | bytes 1179656 | tf_op jit(solution)/shard_map/ppermute | solution.py:42
  181.5 16.4 %slice-start.2 = ((s8[6291456]{0:T(1024)(128)(4,1)}), s8[4194304]{0:T(1024)(128)(4,1)S(1)}, s32[]{:S(2)}) async-start(s8[6291456]{0:T(1024)(128)(4,1)} %bitcast.170), calls=%async_computation.2 | async-start | bytes 8388608
  185.4 6.9 %copy-start.28 = (bf16[4,256,768]{2,1,0:T(8,128)(2,1)S(1)}, bf16[4,256,768]{2,1,0:T(8,128)(2,1)}, u32[]{:S(2)}) copy-start(bf16[4,256,768]{2,1,0:T(8,128)(2,1)} %get-tuple-element.37) | copy-start | bytes 4718596
  185.4 12.4 %slice-start.3 = ((s8[6291456]{0:T(1024)(128)(4,1)}), s8[2097152]{0:T(1024)(128)(4,1)S(1)}, s32[]{:S(2)}) async-start(s8[6291456]{0:T(1024)(128)(4,1)} %bitcast.170), calls=%async_computation.3 | async-start | bytes 4194304
  195.3 2.6 copy-start.11
  197.8 7.1 %copy-start.10 = (bf16[1,4,4,96,768]{4,3,2,1,0:T(8,128)(2,1)S(1)}, bf16[1,4,4,96,768]{4,3,2,1,0:T(8,128)(2,1)}, u32[]{:S(2)}) copy-start(bf16[1,4,4,96,768]{4,3,2,1,0:T(8,128)(2,1)} %get-tuple-element.102) | copy-start | bytes 7077892
  197.8 43.9 %collective-permute-start.3 = (bf16[2,1536,768]{2,1,0:T(8,128)(2,1)}, bf16[2,1536,768]{2,1,0:T(8,128)(2,1)}, u32[]{:S(2)}, u32[]{:S(2)}) collective-permute-start(bf16[2,1536,768]{2,1,0:T(8,128)(2,1)} %pad_maximum_fusion), channel_id=1, source_target_pairs={{0,1},{1,0},{2,3},{3,2},{4,5},{5,4},{6,7},{7,6},{8,9},{9,8},{10,11... | collective-permute-start | bytes 14155784 | tf_op jit(solution)/shard_map/ppermute | solution.py:46
  204.9 2.6 copy-start.31
  204.9 2.8 copy-start.13
  211.5 21.2 %collective-permute-start.6 = (bf16[256,768]{1,0:T(8,128)(2,1)}, bf16[256,768]{1,0:T(8,128)(2,1)}, u32[]{:S(2)}, u32[]{:S(2)}) collective-permute-start(bf16[256,768]{1,0:T(8,128)(2,1)} %get-tuple-element.112), channel_id=1, source_target_pairs={{0,6},{1,7},{2,4},{3,5},{4,2},{5,3},{6,0},{7,1},{8,14},{9,15},{10,... | collective-permute-start | bytes 1179656 | tf_op jit(solution)/shard_map/ppermute | solution.py:42
  212.1 9.5 %copy-start.29 = (bf16[4,256,768]{2,1,0:T(8,128)(2,1)S(1)}, bf16[4,256,768]{2,1,0:T(8,128)(2,1)}, u32[]{:S(2)}) copy-start(bf16[4,256,768]{2,1,0:T(8,128)(2,1)} %get-tuple-element.37) | copy-start | bytes 4718596
  212.1 9.5 %copy-start.32 = (bf16[1024,1536]{1,0:T(8,128)(2,1)S(1)}, bf16[1024,1536]{1,0:T(8,128)(2,1)}, u32[]{:S(2)}) copy-start(bf16[1024,1536]{1,0:T(8,128)(2,1)} %copy-done.31) | copy-start | bytes 9437188
  226.4 11.6 %collective-permute-start.5 = (bf16[256,768]{1,0:T(8,128)(2,1)}, bf16[256,768]{1,0:T(8,128)(2,1)}, u32[]{:S(2)}, u32[]{:S(2)}) collective-permute-start(bf16[256,768]{1,0:T(8,128)(2,1)} %get-tuple-element.113), channel_id=1, source_target_pairs={{0,4},{1,5},{2,6},{3,7},{4,0},{5,1},{6,2},{7,3},{8,12},{9,13},{10,... | collective-permute-start | bytes 1179656 | tf_op jit(solution)/shard_map/ppermute | solution.py:42
  228.0 11.3 %collective-permute-start.4 = (bf16[256,768]{1,0:T(8,128)(2,1)}, bf16[256,768]{1,0:T(8,128)(2,1)}, u32[]{:S(2)}, u32[]{:S(2)}) collective-permute-start(bf16[256,768]{1,0:T(8,128)(2,1)} %get-tuple-element.114), channel_id=1, source_target_pairs={{0,2},{1,3},{2,0},{3,1},{4,6},{5,7},{6,4},{7,5},{8,10},{9,11},{10,... | collective-permute-start | bytes 1179656 | tf_op jit(solution)/shard_map/ppermute | solution.py:42
  229.9 9.4 %copy-start.15 = (bf16[256,768]{1,0:T(8,128)(2,1)S(1)}, bf16[256,768]{1,0:T(8,128)(2,1)}, u32[]{:S(2)}) copy-start(bf16[256,768]{1,0:T(8,128)(2,1)} %get-tuple-element.111) | copy-start | bytes 1179652
  229.9 11.9 %copy-start.9 = (f32[1,1536,768]{2,1,0:T(8,128)S(1)}, f32[1,1536,768]{2,1,0:T(8,128)}, u32[]{:S(2)}) copy-start(f32[1,1536,768]{2,1,0:T(8,128)} %convolution_bitcast_fusion) | copy-start | bytes 14155780
  241.7 7.2 %copy-start.16 = (bf16[1024,768]{1,0:T(8,128)(2,1)S(1)}, bf16[1024,768]{1,0:T(8,128)(2,1)}, u32[]{:S(2)}) copy-start(bf16[1024,768]{1,0:T(8,128)(2,1)} %pad_maximum_fusion.1) | copy-start | bytes 4718596
  248.9 3.6 copy-start.20
  251.7 2.9 copy-start.1
  251.8 2.9 copy-start.5
  251.8 2.9 copy-start.7
  280.0 5.3 %copy-start.26 = (s32[32]{0:T(128)S(1)}, s32[32]{0:T(128)}, u32[]{:S(2)}) copy-start(s32[32]{0:T(128)} %copy-done.25) | copy-start | bytes 388
  286.4 42.0 %slice-start = ((s8[4915200]{0:T(1024)(128)(4,1)}), s8[4194304]{0:T(1024)(128)(4,1)S(1)}, s32[]{:S(2)}) async-start(s8[4915200]{0:T(1024)(128)(4,1)} %bitcast.117), calls=%async_computation | async-start | bytes 8388608
  288.4 40.0 %slice-start.1 = ((s8[4915200]{0:T(1024)(128)(4,1)}), s8[720896]{0:T(1024)(128)(4,1)S(1)}, s32[]{:S(2)}) async-start(s8[4915200]{0:T(1024)(128)(4,1)} %bitcast.117), calls=%async_computation.1 | async-start | bytes 1441792
  288.4 40.0 %collective-permute-start.7 = (bf16[384,3200]{1,0:T(8,128)(2,1)S(1)}, bf16[384,3200]{1,0:T(8,128)(2,1)S(1)}, u32[]{:S(2)}, u32[]{:S(2)}) collective-permute-start(bf16[384,3200]{1,0:T(8,128)(2,1)S(1)} %slice.375), channel_id=1, source_target_pairs={{0,1},{1,0},{2,3},{3,2},{4,5},{5,4},{6,7},{7,6},{8,9},{9,8},{10,11... | collective-permute-start | bytes 7372808 | tf_op jit(solution)/shard_map/ppermute | solution.py:46
  290.4 2.1 collective-permute-start.14
  291.1 27.4 %collective-permute-start.17 = (bf16[2,384,768]{2,1,0:T(8,128)(2,1)S(1)}, bf16[2,384,768]{2,1,0:T(8,128)(2,1)S(1)}, u32[]{:S(2)}, u32[]{:S(2)}) collective-permute-start(bf16[2,384,768]{2,1,0:T(8,128)(2,1)S(1)} %get-tuple-element.99), channel_id=1, source_target_pairs={{24,16},{25,17},{26,18},{27,19},{28,20},{29,21},{30,22},{31,23}} | collective-permute-start | bytes 3538952 | tf_op jit(solution)/shard_map/ppermute | solution.py:53
  321.7 13.4 %collective-permute-start.15 = (bf16[2,384,768]{2,1,0:T(8,128)(2,1)}, bf16[2,384,768]{2,1,0:T(8,128)(2,1)S(1)}, u32[]{:S(2)}, u32[]{:S(2)}) collective-permute-start(bf16[2,384,768]{2,1,0:T(8,128)(2,1)} %get-tuple-element.96), channel_id=1, source_target_pairs={{0,8},{1,9},{2,10},{3,11},{4,12},{5,13},{6,14},{7,15},{8,16},{9,17... | collective-permute-start | bytes 3538952 | tf_op jit(solution)/shard_map/ppermute | solution.py:53
  322.4 30.5 %collective-permute-start.18 = (bf16[2,384,768]{2,1,0:T(8,128)(2,1)}, bf16[2,384,768]{2,1,0:T(8,128)(2,1)}, u32[]{:S(2)}, u32[]{:S(2)}) collective-permute-start(bf16[2,384,768]{2,1,0:T(8,128)(2,1)} %get-tuple-element.97), channel_id=1, source_target_pairs={{16,8},{17,9},{18,10},{19,11},{20,12},{21,13},{22,14},{23,15},{24,... | collective-permute-start | bytes 3538952 | tf_op jit(solution)/shard_map/ppermute | solution.py:53
  329.0 1.4 copy-start.8
  331.6 32.3 %collective-permute-start.10 = (bf16[96,3200]{1,0:T(8,128)(2,1)}, bf16[96,3200]{1,0:T(8,128)(2,1)}, u32[]{:S(2)}, u32[]{:S(2)}) collective-permute-start(bf16[96,3200]{1,0:T(8,128)(2,1)} %get-tuple-element.105), channel_id=1, source_target_pairs={{0,6},{1,7},{2,4},{3,5},{4,2},{5,3},{6,0},{7,1},{8,14},{9,15},{10,... | collective-permute-start | bytes 1843208 | tf_op jit(solution)/shard_map/ppermute | solution.py:42
  333.0 30.9 %collective-permute-start.9 = (bf16[96,3200]{1,0:T(8,128)(2,1)}, bf16[96,3200]{1,0:T(8,128)(2,1)}, u32[]{:S(2)}, u32[]{:S(2)}) collective-permute-start(bf16[96,3200]{1,0:T(8,128)(2,1)} %get-tuple-element.106), channel_id=1, source_target_pairs={{0,4},{1,5},{2,6},{3,7},{4,0},{5,1},{6,2},{7,3},{8,12},{9,13},{10,... | collective-permute-start | bytes 1843208 | tf_op jit(solution)/shard_map/ppermute | solution.py:42
  334.5 29.3 %collective-permute-start.8 = (bf16[96,3200]{1,0:T(8,128)(2,1)S(1)}, bf16[96,3200]{1,0:T(8,128)(2,1)}, u32[]{:S(2)}, u32[]{:S(2)}) collective-permute-start(bf16[96,3200]{1,0:T(8,128)(2,1)S(1)} %get-tuple-element.104), channel_id=1, source_target_pairs={{0,2},{1,3},{2,0},{3,1},{4,6},{5,7},{6,4},{7,5},{8,10},{9,11},{10,... | collective-permute-start | bytes 1843208 | tf_op jit(solution)/shard_map/ppermute | solution.py:42
  356.9 15.3 %copy-start.3 = (f32[416,768]{1,0:T(8,128)S(1)}, f32[416,768]{1,0:T(8,128)}, u32[]{:S(2)}) copy-start(f32[416,768]{1,0:T(8,128)} %copy-done.2) | copy-start | bytes 3833860
  356.9 15.4 %copy-start.17 = (bf16[1024,768]{1,0:T(8,128)(2,1)S(1)}, bf16[1024,768]{1,0:T(8,128)(2,1)}, u32[]{:S(2)}) copy-start(bf16[1024,768]{1,0:T(8,128)(2,1)} %pad_maximum_fusion.1) | copy-start | bytes 4718596
  356.9 15.4 %copy-start.34 = (f32[416]{0:T(512)S(1)}, f32[416]{0:T(512)}, u32[]{:S(2)}) copy-start(f32[416]{0:T(512)} %copy-done.33) | copy-start | bytes 4996
  356.9 15.4 %copy-start.36 = (f32[416]{0:T(512)S(1)}, f32[416]{0:T(512)}, u32[]{:S(2)}) copy-start(f32[416]{0:T(512)} %copy-done.35) | copy-start | bytes 4996
  356.9 52.0 %collective-permute-start.19 = (bf16[2,384,768]{2,1,0:T(8,128)(2,1)}, bf16[2,384,768]{2,1,0:T(8,128)(2,1)}, u32[]{:S(2)}, u32[]{:S(2)}) collective-permute-start(bf16[2,384,768]{2,1,0:T(8,128)(2,1)} %get-tuple-element.95), channel_id=1, source_target_pairs={{8,0},{9,1},{10,2},{11,3},{12,4},{13,5},{14,6},{15,7},{16,8},{17,9... | collective-permute-start | bytes 3538952 | tf_op jit(solution)/shard_map/ppermute | solution.py:53
  362.6 46.4 %collective-permute-start.16 = (bf16[2,384,768]{2,1,0:T(8,128)(2,1)}, bf16[2,384,768]{2,1,0:T(8,128)(2,1)}, u32[]{:S(2)}, u32[]{:S(2)}) collective-permute-start(bf16[2,384,768]{2,1,0:T(8,128)(2,1)} %get-tuple-element.94), channel_id=1, source_target_pairs={{0,8},{1,9},{2,10},{3,11},{4,12},{5,13},{6,14},{7,15},{8,16},{9,17... | collective-permute-start | bytes 3538952 | tf_op jit(solution)/shard_map/ppermute | solution.py:53
  366.6 28.7 %collective-permute-start.13 = (bf16[24,3200]{1,0:T(8,128)(2,1)}, bf16[24,3200]{1,0:T(8,128)(2,1)S(1)}, u32[]{:S(2)}, u32[]{:S(2)}) collective-permute-start(bf16[24,3200]{1,0:T(8,128)(2,1)} %get-tuple-element.123), channel_id=1, source_target_pairs={{0,8},{1,9},{2,10},{3,11},{4,12},{5,13},{6,14},{7,15},{8,16},{9,17... | collective-permute-start | bytes 460808 | tf_op jit(solution)/shard_map/ppermute | solution.py:57
  370.5 34.5 %collective-permute-start.12 = (bf16[24,3200]{1,0:T(8,128)(2,1)}, bf16[24,3200]{1,0:T(8,128)(2,1)}, u32[]{:S(2)}, u32[]{:S(2)}) collective-permute-start(bf16[24,3200]{1,0:T(8,128)(2,1)} %get-tuple-element.124), channel_id=1, source_target_pairs={{0,16},{1,17},{2,18},{3,19},{4,20},{5,21},{6,22},{7,23},{8,24},{9,... | collective-permute-start | bytes 460808 | tf_op jit(solution)/shard_map/ppermute | solution.py:57
  370.7 34.3 %collective-permute-start.11 = (bf16[24,3200]{1,0:T(8,128)(2,1)S(1)}, bf16[24,3200]{1,0:T(8,128)(2,1)}, u32[]{:S(2)}, u32[]{:S(2)}) collective-permute-start(bf16[24,3200]{1,0:T(8,128)(2,1)S(1)} %get-tuple-element.122), channel_id=1, source_target_pairs={{0,24},{1,25},{2,26},{3,27},{4,28},{5,29},{6,30},{7,31},{8,0},{9,1... | collective-permute-start | bytes 460808 | tf_op jit(solution)/shard_map/ppermute | solution.py:57
  411.4 10.4 %collective-permute-start.20 = (bf16[2,96,768]{2,1,0:T(8,128)(2,1)S(1)}, bf16[2,96,768]{2,1,0:T(8,128)(2,1)S(1)}, u32[]{:S(2)}, u32[]{:S(2)}) collective-permute-start(bf16[2,96,768]{2,1,0:T(8,128)(2,1)S(1)} %get-tuple-element.121), channel_id=1, source_target_pairs={{0,6},{1,7},{2,4},{3,5},{4,2},{5,3},{6,0},{7,1},{8,14},{9,15},{10,... | collective-permute-start | bytes 884744 | tf_op jit(solution)/shard_map/ppermute | solution.py:42
  412.9 11.8 %collective-permute-start.21 = (bf16[2,96,768]{2,1,0:T(8,128)(2,1)S(1)}, bf16[2,96,768]{2,1,0:T(8,128)(2,1)S(1)}, u32[]{:S(2)}, u32[]{:S(2)}) collective-permute-start(bf16[2,96,768]{2,1,0:T(8,128)(2,1)S(1)} %get-tuple-element.120), channel_id=1, source_target_pairs={{0,4},{1,5},{2,6},{3,7},{4,0},{5,1},{6,2},{7,3},{8,12},{9,13},{10,... | collective-permute-start | bytes 884744 | tf_op jit(solution)/shard_map/ppermute | solution.py:42
  414.7 10.0 %collective-permute-start.22 = (bf16[2,96,768]{2,1,0:T(8,128)(2,1)S(1)}, bf16[2,96,768]{2,1,0:T(8,128)(2,1)S(1)}, u32[]{:S(2)}, u32[]{:S(2)}) collective-permute-start(bf16[2,96,768]{2,1,0:T(8,128)(2,1)S(1)} %get-tuple-element.119), channel_id=1, source_target_pairs={{0,2},{1,3},{2,0},{3,1},{4,6},{5,7},{6,4},{7,5},{8,10},{9,11},{10,... | collective-permute-start | bytes 884744 | tf_op jit(solution)/shard_map/ppermute | solution.py:42
